TPU v7x, 32 devices: a whole 2x2x4 slice. The times are simulated.
32 devices in a mesh: dp: 8 (over z, x), head: 4 (over y, core).
Axes of the slice: x: 2, y: 2, z: 4, core: 2. Of those that a mesh axis runs over, the one named last changes fastest.
Arguments:
- inputs: bfloat16 [16384, 768], P(('dp', 'head')), may hold values from -6 to 6
- cotangent: bfloat16 [16384, 768], P(('dp', 'head')), may hold values from -6 to 6
- lengths: int32 [32], replicated, may hold values from 1 to 8192, 16128 in all
- w_qkv: float32 [2, 768, 2304], P(None, 'dp', 'head'), may hold values from -0.21875 to 0.21875
- m_qkv: float32 [2, 768, 2304], P(None, 'dp', 'head'), may hold values from -0.0004272461 to 0.0004272461
- v_qkv: float32 [2, 768, 2304], P(None, 'dp', 'head'), may hold values from 7.061189e-11 to 2.8244757e-10
- w_out: float32 [2, 768, 768], P(None, 'dp', 'head'), may hold values from -2.5 to 2.5
- m_out: float32 [2, 768, 768], P(None, 'dp', 'head'), may hold values from -0.0004272461 to 0.0004272461
- v_out: float32 [2, 768, 768], P(None, 'dp', 'head'), may hold values from 8.826486e-12 to 3.5305946e-11
- w_up: float32 [2, 768, 3072], P(None, 'dp', 'head'), may hold values from -0.21875 to 0.21875
- m_up: float32 [2, 768, 3072], P(None, 'dp', 'head'), may hold values from -0.0004272461 to 0.0004272461
- v_up: float32 [2, 768, 3072], P(None, 'dp', 'head'), may hold values from 7.061189e-11 to 2.8244757e-10
- w_down: float32 [2, 3072, 768], P(None, 'dp', 'head'), may hold values from -0.109375 to 0.109375
- m_down: float32 [2, 3072, 768], P(None, 'dp', 'head'), may hold values from -0.0004272461 to 0.0004272461
- v_down: float32 [2, 3072, 768], P(None, 'dp', 'head'), may hold values from 7.061189e-11 to 2.8244757e-10
- norm_params: float32 [2, 4, 768], P(None, 'head', 'dp'), may hold values from -0.8 to 2.4
- m_norm: float32 [2, 4, 768], P(None, 'head', 'dp'), may hold values from -0.0014648438 to 0.0014648438
- v_norm: float32 [2, 4, 768], P(None, 'head', 'dp'), may hold values from 7.0611894e-10 to 2.8244758e-09
Outputs:
- output: float32 [16384, 768], P(('dp', 'head'))
- grad_input: float32 [16384, 768], P(('dp', 'head'))
- grad_norm: float32 [1], replicated
- new_w_qkv: float32 [2, 768, 2304], P(None, 'dp', 'head')
- new_m_qkv: float32 [2, 768, 2304], P(None, 'dp', 'head')
- new_v_qkv: float32 [2, 768, 2304], P(None, 'dp', 'head')
- new_w_out: float32 [2, 768, 768], P(None, 'dp', 'head')
- new_m_out: float32 [2, 768, 768], P(None, 'dp', 'head')
- new_v_out: float32 [2, 768, 768], P(None, 'dp', 'head')
- new_w_up: float32 [2, 768, 3072], P(None, 'dp', 'head')
- new_m_up: float32 [2, 768, 3072], P(None, 'dp', 'head')
- new_v_up: float32 [2, 768, 3072], P(None, 'dp', 'head')
- new_w_down: float32 [2, 3072, 768], P(None, 'dp', 'head')
- new_m_down: float32 [2, 3072, 768], P(None, 'dp', 'head')
- new_v_down: float32 [2, 3072, 768], P(None, 'dp', 'head')
- new_norm: float32 [2, 4, 768], P(None, 'head', 'dp')
- new_m_norm: float32 [2, 4, 768], P(None, 'head', 'dp')
- new_v_norm: float32 [2, 4, 768], P(None, 'head', 'dp')
Inputs may be any that keep to these rules, and one draw needn't show every extreme that they name: The lengths sum to 16128; the rows after them are padding; the largest is exactly 8192.
All inputs are finite; a program needn't handle non-finite values.
Results may differ from a plain program's by a relative error of at most 0.019.
Values may be sent and summed in bfloat16 or wider, within the bound.
A program may use at most 256 MiB of HBM per device.

v0:
```python
import math

import jax
import jax.numpy as jnp
from jax import lax
from jax.sharding import PartitionSpec as P

HEADS = 12
L = 2
LONGEST = 8192


exact_mode = lax.Precision.HIGHEST
beta_one = 0.9
beta_two = 0.999
adam_eps = 1e-08
decay_rate = 0.1
rate_matrix = 0.1
rate_outproj = 0.5
rate_norm = 0.5
clip_limit = 1.0
norm_eps = 1e-05
step_fixed = 10.0


def carried_in(shard, axis, join, neutral):
    place = lax.axis_index(axis)
    gathered = jax.tree.map(
        lambda a, kind: lax.all_gather(a.astype(kind), axis),
        shard,
        (jnp.bfloat16, jnp.bfloat16, jnp.bfloat16, jnp.bfloat16, jnp.bfloat16),
    )
    state = jax.tree.map(lambda a, e: jnp.zeros_like(a) + jnp.asarray(e, a.dtype), shard, neutral)

    def one(step, state):
        return join(
            state,
            jax.tree.map(
                lambda a, own: lax.dynamic_index_in_dim(a, step, 0, False).astype(own.dtype),
                gathered,
                shard,
            ),
        )

    return lax.fori_loop(0, place, one, state)


def carried_in_2(shard, axis, combine, identity):
    length, index = (lax.axis_size(axis), lax.axis_index(axis))
    everything = jax.tree.map(
        lambda part, kind: lax.all_gather(part.astype(kind), axis),
        shard,
        jax.tree.map(lambda a: jnp.bfloat16 if a.dtype == jnp.float32 else a.dtype, shard),
    )
    start = jax.tree.map(
        lambda part, zero: jnp.broadcast_to(jnp.asarray(zero, part.dtype), part.shape),
        shard,
        identity,
    )

    def step(k, before):
        at = length - 1 - k
        reached = at > index
        new = combine(
            before, jax.tree.map(lambda part, own: part[at].astype(own.dtype), everything, shard)
        )
        return jax.tree.map(lambda a, b: jnp.where(reached, a, b), new, before)

    return lax.fori_loop(0, length, step, start)


def stream_meta(lengths, first_row, row_count):
    seq_count = lengths.shape[0]
    seq_ends = jnp.cumsum(lengths, dtype=jnp.int32)
    seq_starts = seq_ends - lengths
    row_ids = first_row + jnp.arange(row_count, dtype=jnp.int32)
    begun = seq_starts[None, :] <= row_ids[:, None]
    seg_raw = jnp.sum(begun.astype(jnp.int32), axis=1, dtype=jnp.int32) - 1
    seg_start = jnp.max(jnp.where(begun, seq_starts[None, :], 0), axis=1)
    inside = row_ids < seq_ends[seq_count - 1]
    seg_ids = jnp.where(inside, seg_raw, seq_count)
    offsets = jnp.where(inside, row_ids - seg_start, 0).astype(jnp.float32)
    angles = offsets * (0.5 * math.pi / LONGEST)
    return (seg_ids, jnp.cos(angles), jnp.sin(angles), inside.astype(jnp.float32))


def block_step(carry_in, block_data):
    state_cos, state_sin, sum_cos, sum_sin, carry_seg = carry_in
    queries, key_rows, value_rows, seg_ids, cos_row, sin_row = block_data
    block_len = seg_ids.shape[0]
    position_ids = jnp.arange(block_len, dtype=jnp.int32)
    allowed = (seg_ids[:, None] == seg_ids[None, :]) & (
        position_ids[None, :] <= position_ids[:, None]
    )
    closeness = cos_row[:, None] * cos_row[None, :] + sin_row[:, None] * sin_row[None, :]
    weight_map = jnp.where(allowed, closeness, 0.0)
    query_low = queries.astype(jnp.bfloat16)
    key_low = key_rows.astype(jnp.bfloat16)
    value_low = value_rows.astype(jnp.bfloat16)
    raw_scores = jnp.einsum("ihe,jhe->hij", query_low, key_low, preferred_element_type=jnp.float32)
    scores_low = (raw_scores * weight_map[None]).astype(jnp.bfloat16)
    numerator = jnp.einsum(
        "hij,jhe->ihe", scores_low, value_low, preferred_element_type=jnp.float32
    )
    denominator = jnp.transpose(jnp.sum(scores_low.astype(jnp.float32), axis=2))
    following = (seg_ids == carry_seg).astype(jnp.float32)
    q_cos = queries * (cos_row * following)[:, None, None]
    q_sin = queries * (sin_row * following)[:, None, None]
    numerator = (
        numerator
        + jnp.einsum("ihe,hef->ihf", q_cos, state_cos, precision=exact_mode)
        + jnp.einsum("ihe,hef->ihf", q_sin, state_sin, precision=exact_mode)
    )
    denominator = (
        denominator
        + jnp.einsum("ihe,he->ih", q_cos, sum_cos, precision=exact_mode)
        + jnp.einsum("ihe,he->ih", q_sin, sum_sin, precision=exact_mode)
    )
    last_seg = seg_ids[block_len - 1]
    in_last = (seg_ids == last_seg).astype(jnp.float32)
    k_cos = key_rows * (cos_row * in_last)[:, None, None]
    k_sin = key_rows * (sin_row * in_last)[:, None, None]
    keep_old = (carry_seg == last_seg).astype(jnp.float32)
    state_cos = keep_old * state_cos + jnp.einsum(
        "jhe,jhf->hef", k_cos, value_rows, precision=exact_mode
    )
    state_sin = keep_old * state_sin + jnp.einsum(
        "jhe,jhf->hef", k_sin, value_rows, precision=exact_mode
    )
    sum_cos = keep_old * sum_cos + jnp.sum(k_cos, axis=0)
    sum_sin = keep_old * sum_sin + jnp.sum(k_sin, axis=0)
    return ((state_cos, state_sin, sum_cos, sum_sin, last_seg), (numerator, denominator))


def run_blocks(queries, key_rows, value_rows, seg_ids, cos_row, sin_row, block_len):
    row_count, head_count, head_dim = queries.shape
    block_count = row_count // block_len

    def by_blocks(array):
        return array.reshape((block_count, block_len) + array.shape[1:])

    zero_state = jnp.zeros((head_count, head_dim, head_dim), jnp.float32)
    zero_sum = jnp.zeros((head_count, head_dim), jnp.float32)
    initial = (zero_state, zero_state, zero_sum, zero_sum, jnp.array(-1, jnp.int32))
    final_carry, results = lax.scan(
        jax.checkpoint(block_step),
        initial,
        (
            by_blocks(queries),
            by_blocks(key_rows),
            by_blocks(value_rows),
            by_blocks(seg_ids),
            by_blocks(cos_row),
            by_blocks(sin_row),
        ),
    )
    numerator = results[0].reshape(row_count, head_count, head_dim)
    denominator = results[1].reshape(row_count, head_count)
    return (
        (final_carry[0], final_carry[1], final_carry[2], final_carry[3]),
        numerator,
        denominator,
    )


def finish_rows(queries, numerator, denominator, state, following, cos_row, sin_row):
    state_cos, state_sin, sum_cos, sum_sin = state
    q_cos = queries * (cos_row * following)[:, None, None]
    q_sin = queries * (sin_row * following)[:, None, None]
    numerator = (
        numerator
        + jnp.einsum("ihe,hef->ihf", q_cos, state_cos, precision=exact_mode)
        + jnp.einsum("ihe,hef->ihf", q_sin, state_sin, precision=exact_mode)
    )
    denominator = (
        denominator
        + jnp.einsum("ihe,he->ih", q_cos, sum_cos, precision=exact_mode)
        + jnp.einsum("ihe,he->ih", q_sin, sum_sin, precision=exact_mode)
    )
    return numerator / jnp.maximum(denominator, 1.0)[:, :, None]


def chain_combine(earlier, later):
    keep_old = 1.0 - later[0]
    return (
        jnp.maximum(earlier[0], later[0]),
        later[1] + keep_old * earlier[1],
        later[2] + keep_old * earlier[2],
        later[3] + keep_old * earlier[3],
        later[4] + keep_old * earlier[4],
    )


def layer_norm(inputs_row, gain_row, shift_row):
    mean_row = jnp.mean(inputs_row, axis=-1, keepdims=True)
    centered = inputs_row - mean_row
    variance = jnp.mean(centered * centered, axis=-1, keepdims=True)
    return centered * lax.rsqrt(variance + norm_eps) * gain_row + shift_row


def gelu_exact(inner_pre):
    return jax.nn.gelu(inner_pre, approximate=False)


def contract_rows(left, right):
    return lax.dot_general(
        left, right, (((0,), (0,)), ((), ())), preferred_element_type=jnp.float32
    )


def contract_cols(left, right):
    return lax.dot_general(
        left, right, (((1,), (1,)), ((), ())), preferred_element_type=jnp.float32
    )


def exact_rows(left, right):
    return lax.dot_general(
        left,
        right,
        (((0,), (0,)), ((), ())),
        precision=exact_mode,
        preferred_element_type=jnp.float32,
    )


def exact_cols(left, right):
    return lax.dot_general(
        left,
        right,
        (((1,), (1,)), ((), ())),
        precision=exact_mode,
        preferred_element_type=jnp.float32,
    )


def adam_step(weight, first_old, second_old, gradient, factor, step_rate, decay_coef):
    clipped = gradient * factor
    first_new = beta_one * first_old + (1.0 - beta_one) * clipped
    second_new = beta_two * second_old + (1.0 - beta_two) * clipped * clipped
    first_hat = first_new / (1.0 - beta_one**step_fixed)
    second_hat = second_new / (1.0 - beta_two**step_fixed)
    weight_new = weight - step_rate * (
        first_hat / (jnp.sqrt(second_hat) + adam_eps) + decay_coef * weight
    )
    return (weight_new, first_new, second_new)


def body(
    inputs,
    cotangent,
    lengths,
    w_qkv,
    m_qkv,
    v_qkv,
    w_out,
    m_out,
    v_out,
    w_up,
    m_up,
    v_up,
    w_down,
    m_down,
    v_down,
    norm_params,
    m_norm,
    v_norm,
):
    tok_rows, model_width = inputs.shape
    groups = lax.axis_size("head")
    group_rows = tok_rows * groups
    group_cols = model_width // groups
    local_heads = HEADS // groups
    head_dim = model_width // HEADS
    block_len = min(512, group_rows)
    first_row = lax.axis_index("dp") * group_rows
    seg_ids, cos_row, sin_row, valid_row = stream_meta(lengths, first_row, group_rows)
    prev_seg = stream_meta(lengths, first_row - 1, 1)[0][0]
    following = (seg_ids == prev_seg).astype(jnp.float32)
    reset_flag = (seg_ids[group_rows - 1] != prev_seg).astype(jnp.float32)
    zero_state = jnp.zeros((local_heads, head_dim, head_dim), jnp.float32)
    zero_sum = jnp.zeros((local_heads, head_dim), jnp.float32)
    identity = (jnp.zeros((), jnp.float32), zero_state, zero_state, zero_sum, zero_sum)

    def local_blocks(queries, key_rows, value_rows):
        return run_blocks(queries, key_rows, value_rows, seg_ids, cos_row, sin_row, block_len)

    def finish_local(queries, numerator, denominator, state):
        return finish_rows(queries, numerator, denominator, state, following, cos_row, sin_row)

    hidden = inputs.astype(jnp.float32)
    kept_layers = []
    for layer_idx in range(L):
        shards = (
            lax.all_gather(w_qkv[layer_idx].astype(jnp.bfloat16), "head", axis=1, tiled=True),
            lax.all_gather(w_out[layer_idx].astype(jnp.bfloat16), "head", axis=1, tiled=True),
            lax.all_gather(w_up[layer_idx].astype(jnp.bfloat16), "head", axis=1, tiled=True),
            lax.all_gather(w_down[layer_idx].astype(jnp.bfloat16), "head", axis=1, tiled=True),
            lax.all_gather(norm_params[layer_idx].astype(jnp.bfloat16), "head", axis=0, tiled=True),
        )
        weights = (
            lax.all_gather(shards[0], "dp", axis=0, tiled=True),
            lax.all_gather(shards[1], "dp", axis=0, tiled=True),
            lax.all_gather(shards[2], "dp", axis=0, tiled=True),
            lax.all_gather(shards[3], "dp", axis=0, tiled=True),
            lax.all_gather(shards[4], "dp", axis=1, tiled=True),
        )
        qkv_w, out_w, up_w, down_w, norm_low = weights
        norm_rows = norm_low.astype(jnp.float32)
        acts_low = hidden.astype(jnp.bfloat16)
        mixed_rows = jnp.dot(acts_low, qkv_w, preferred_element_type=jnp.float32)
        positive = jnp.concatenate(
            [jax.nn.softplus(mixed_rows[:, : 2 * model_width]), mixed_rows[:, 2 * model_width :]],
            axis=1,
        )
        outgoing = positive.astype(jnp.bfloat16).reshape(tok_rows, 3, groups, group_cols)
        incoming = lax.all_to_all(outgoing, "head", split_axis=2, concat_axis=0, tiled=True)
        incoming = incoming.reshape(group_rows, 3, local_heads, head_dim).astype(jnp.float32)
        queries = incoming[:, 0]
        key_rows = incoming[:, 1] * valid_row[:, None, None]
        value_rows = incoming[:, 2]
        summary, numerator, denominator = local_blocks(queries, key_rows, value_rows)
        carried = carried_in(
            (reset_flag, summary[0], summary[1], summary[2], summary[3]),
            "dp",
            chain_combine,
            identity,
        )
        state_in = (carried[1], carried[2], carried[3], carried[4])
        attended = finish_local(queries, numerator, denominator, state_in)
        sent_back = attended.astype(jnp.bfloat16).reshape(group_rows, 1, group_cols)
        attended_rows = lax.all_to_all(
            sent_back, "head", split_axis=0, concat_axis=1, tiled=True
        ).reshape(tok_rows, model_width)
        first_in = hidden + jnp.dot(attended_rows, out_w, preferred_element_type=jnp.float32)
        first_out = layer_norm(first_in, norm_rows[0], norm_rows[1])
        first_low = first_out.astype(jnp.bfloat16)
        inner_pre = jnp.dot(first_low, up_w, preferred_element_type=jnp.float32)
        activated = gelu_exact(inner_pre).astype(jnp.bfloat16)
        second_in = first_out + jnp.dot(activated, down_w, preferred_element_type=jnp.float32)
        kept_layers.append(
            (
                acts_low,
                weights,
                mixed_rows,
                queries,
                key_rows,
                value_rows,
                numerator,
                denominator,
                state_in,
                attended_rows,
                first_in,
                first_low,
                inner_pre,
                activated,
                second_in,
            )
        )
        hidden = layer_norm(second_in, norm_rows[2], norm_rows[3])
    grad_hidden = cotangent.astype(jnp.float32)
    layer_grads = []
    for layer_idx in reversed(range(L)):
        (
            acts_low,
            weights,
            mixed_rows,
            queries,
            key_rows,
            value_rows,
            numerator,
            denominator,
            state_in,
            attended_rows,
            first_in,
            first_low,
            inner_pre,
            activated,
            second_in,
        ) = kept_layers[layer_idx]
        qkv_w, out_w, up_w, down_w, norm_low = weights
        norm_rows = norm_low.astype(jnp.float32)
        _, norm_pull_two = jax.vjp(layer_norm, second_in, norm_rows[2], norm_rows[3])
        grad_second, grad_gain_two, grad_shift_two = norm_pull_two(grad_hidden)
        grad_branch_two = grad_second.astype(jnp.bfloat16)
        grad_down = contract_rows(activated, grad_branch_two)
        grad_activated = contract_cols(grad_branch_two, down_w)
        _, gelu_pull = jax.vjp(gelu_exact, inner_pre)
        grad_inner = gelu_pull(grad_activated)[0].astype(jnp.bfloat16)
        grad_up = contract_rows(first_low, grad_inner)
        grad_first = grad_second + contract_cols(grad_inner, up_w)
        _, norm_pull_one = jax.vjp(layer_norm, first_in, norm_rows[0], norm_rows[1])
        grad_first_in, grad_gain_one, grad_shift_one = norm_pull_one(grad_first)
        grad_branch = grad_first_in.astype(jnp.bfloat16)
        grad_out = contract_rows(attended_rows, grad_branch)
        grad_attended = (
            contract_cols(grad_branch, out_w)
            .astype(jnp.bfloat16)
            .reshape(tok_rows, groups, group_cols)
        )
        grad_heads = lax.all_to_all(grad_attended, "head", split_axis=1, concat_axis=0, tiled=True)
        grad_heads = grad_heads.reshape(group_rows, local_heads, head_dim).astype(jnp.float32)
        _, finish_pull = jax.vjp(finish_local, queries, numerator, denominator, state_in)
        grad_query_one, grad_numerator, grad_denominator, grad_state = finish_pull(grad_heads)
        grad_summary = carried_in_2(
            (reset_flag, grad_state[0], grad_state[1], grad_state[2], grad_state[3]),
            "dp",
            chain_combine,
            identity,
        )
        _, blocks_pull = jax.vjp(local_blocks, queries, key_rows, value_rows)
        grad_query_two, grad_keys, grad_values = blocks_pull(
            (
                (grad_summary[1], grad_summary[2], grad_summary[3], grad_summary[4]),
                grad_numerator,
                grad_denominator,
            )
        )
        grad_keys = grad_keys * valid_row[:, None, None]
        grad_send = (
            jnp.stack([grad_query_one + grad_query_two, grad_keys, grad_values], axis=1)
            .astype(jnp.bfloat16)
            .reshape(group_rows, 3, 1, group_cols)
        )
        grad_mixed = lax.all_to_all(
            grad_send, "head", split_axis=0, concat_axis=2, tiled=True
        ).reshape(tok_rows, 3 * model_width)
        slope = jnp.concatenate(
            [
                jax.nn.sigmoid(mixed_rows[:, : 2 * model_width]),
                jnp.ones((tok_rows, model_width), jnp.float32),
            ],
            axis=1,
        )
        grad_pre = grad_mixed.astype(jnp.float32) * slope
        grad_qkv = exact_rows(acts_low.astype(jnp.float32), grad_pre)
        grad_hidden = grad_first_in + exact_cols(grad_pre, qkv_w.astype(jnp.float32))
        grad_norm_rows = jnp.stack(
            [grad_gain_one, grad_shift_one, grad_gain_two, grad_shift_two], axis=0
        )
        layer_grads.append((grad_qkv, grad_out, grad_up, grad_down, grad_norm_rows))
    layer_grads = layer_grads[::-1]
    reduced = []
    for layer_idx in range(L):
        grad_set = layer_grads[layer_idx]
        partial_set = (
            lax.psum_scatter(grad_set[0], "dp", scatter_dimension=0, tiled=True),
            lax.psum_scatter(grad_set[1], "dp", scatter_dimension=0, tiled=True),
            lax.psum_scatter(grad_set[2], "dp", scatter_dimension=0, tiled=True),
            lax.psum_scatter(grad_set[3], "dp", scatter_dimension=0, tiled=True),
            lax.psum_scatter(grad_set[4], "dp", scatter_dimension=1, tiled=True),
        )
        final_set = (
            lax.psum_scatter(
                partial_set[0].astype(jnp.bfloat16), "head", scatter_dimension=1, tiled=True
            ).astype(jnp.float32),
            lax.psum_scatter(
                partial_set[1].astype(jnp.bfloat16), "head", scatter_dimension=1, tiled=True
            ).astype(jnp.float32),
            lax.psum_scatter(
                partial_set[2].astype(jnp.bfloat16), "head", scatter_dimension=1, tiled=True
            ).astype(jnp.float32),
            lax.psum_scatter(
                partial_set[3].astype(jnp.bfloat16), "head", scatter_dimension=1, tiled=True
            ).astype(jnp.float32),
            lax.psum_scatter(
                partial_set[4].astype(jnp.bfloat16), "head", scatter_dimension=0, tiled=True
            ).astype(jnp.float32),
        )
        reduced.append(final_set)
    grad_kinds = [
        jnp.stack([reduced[layer_pos][kind_pos] for layer_pos in range(L)], axis=0)
        for kind_pos in range(5)
    ]
    square_sum = jnp.float32(0.0)
    for gradient in grad_kinds:
        square_sum = square_sum + jnp.sum(gradient * gradient)
    total_sum = lax.psum(square_sum, ("dp", "head"))
    grad_norm = jnp.sqrt(total_sum)
    factor = clip_limit / jnp.maximum(grad_norm, clip_limit)
    new_qkv = adam_step(w_qkv, m_qkv, v_qkv, grad_kinds[0], factor, rate_matrix, decay_rate)
    new_out = adam_step(w_out, m_out, v_out, grad_kinds[1], factor, rate_outproj, decay_rate)
    new_up = adam_step(w_up, m_up, v_up, grad_kinds[2], factor, rate_matrix, decay_rate)
    new_down = adam_step(w_down, m_down, v_down, grad_kinds[3], factor, rate_matrix, decay_rate)
    new_norm = adam_step(norm_params, m_norm, v_norm, grad_kinds[4], factor, rate_norm, 0.0)
    return (
        hidden,
        grad_hidden,
        grad_norm.reshape(1),
        new_qkv[0],
        new_qkv[1],
        new_qkv[2],
        new_out[0],
        new_out[1],
        new_out[2],
        new_up[0],
        new_up[1],
        new_up[2],
        new_down[0],
        new_down[1],
        new_down[2],
        new_norm[0],
        new_norm[1],
        new_norm[2],
    )


def solution(mesh):
    in_specs = (
        P(("dp", "head"), None),
        P(("dp", "head"), None),
        P(),
        P(None, "dp", "head"),
        P(None, "dp", "head"),
        P(None, "dp", "head"),
        P(None, "dp", "head"),
        P(None, "dp", "head"),
        P(None, "dp", "head"),
        P(None, "dp", "head"),
        P(None, "dp", "head"),
        P(None, "dp", "head"),
        P(None, "dp", "head"),
        P(None, "dp", "head"),
        P(None, "dp", "head"),
        P(None, "head", "dp"),
        P(None, "head", "dp"),
        P(None, "head", "dp"),
    )
    out_specs = (
        P(("dp", "head"), None),
        P(("dp", "head"), None),
        P(),
        P(None, "dp", "head"),
        P(None, "dp", "head"),
        P(None, "dp", "head"),
        P(None, "dp", "head"),
        P(None, "dp", "head"),
        P(None, "dp", "head"),
        P(None, "dp", "head"),
        P(None, "dp", "head"),
        P(None, "dp", "head"),
        P(None, "dp", "head"),
        P(None, "dp", "head"),
        P(None, "dp", "head"),
        P(None, "head", "dp"),
        P(None, "head", "dp"),
        P(None, "head", "dp"),
    )
    return jax.shard_map(body, mesh=mesh, in_specs=in_specs, out_specs=out_specs, check_vma=False)
```

profile of v0, /device:TPU:0, one launch (start us, length us, event | category | flops | bytes accessed | tf_op | source)
XLA Modules:
  0.0 3159.7 jit_solution(8475958806820524267)
XLA Ops:
  198.5 91.9 %while.240 = (s32[]{:T(128)}, f32[3,64,64]{2,1,0:T(8,128)S(1)}, f32[3,64,64]{2,1,0:T(8,128)S(1)}, f32[3,64]{1,0:T(4,128)}, f32[3,64]{1,0:T(4,128)}, /*index=5*/s...) while((s32[]{:T(128)}, f32[3,64,64]{2,1,0:T(8,128)S(1)}, ...), condition=%wide.region_7.8_spmd.clone, body=%wide.region_3.7_spmd.clone.sunk | while | flops 511939840 | bytes 13335949 | solution.py:145
  290.4 32.0 %all-gather.2 = bf16[24,64,64]{2,1,0:T(8,128)(2,1)S(1)} all-gather(bf16[3,64,64]{2,1,0:T(8,128)(2,1)S(1)} %convert_element_type.887), channel_id=4, replica_groups=mesh['dp'=8,'head'=4] {'dp'}, dimensions={0}, use_global_device_ids=true | all-gather | bytes 221184 | tf_op jit(solution)/shard_map/all_gather | solution.py:29
  322.3 32.4 %all-gather.3 = bf16[24,64,64]{2,1,0:T(8,128)(2,1)S(1)} all-gather(bf16[3,64,64]{2,1,0:T(8,128)(2,1)S(1)} %convert_element_type.891), channel_id=5, replica_groups=mesh['dp'=8,'head'=4] {'dp'}, dimensions={0}, use_global_device_ids=true | all-gather | bytes 221184 | tf_op jit(solution)/shard_map/all_gather | solution.py:29
  434.7 41.5 %all-gather.9 = bf16[4,1,768]{0,1,2:T(2,128)(2,1)S(1)} all-gather(bf16[4,1,96]{0,1,2:T(2,128)(2,1)S(1)} %copy.589), channel_id=11, replica_groups=mesh['dp'=8,'head'=4] {'dp'}, dimensions={2}, use_global_device_ids=true | all-gather | bytes 6912 | tf_op jit(solution)/shard_map/all_gather | solution.py:306
  542.7 32.9 %all-gather.26 = bf16[1,384,768]{1,2,0:T(8,128)(2,1)} all-gather(bf16[1,384,192]{1,2,0:T(8,128)(2,1)S(1)} %get-tuple-element.3543), channel_id=28, replica_groups=mesh['dp'=8,'head'=4] {'head'}, dimensions={2}, use_global_device_ids=true | all-gather | bytes 737280 | tf_op jit(solution)/shard_map/all_gather | solution.py:298
  614.3 101.2 %while.241 = (s32[]{:T(128)}, f32[3,64,64]{2,1,0:T(8,128)S(1)}, f32[3,64,64]{2,1,0:T(8,128)S(1)}, f32[3,64]{1,0:T(4,128)S(1)}, f32[3,64]{1,0:T(4,128)S(1)}, /*in...) while((s32[]{:T(128)}, f32[3,64,64]{2,1,0:T(8,128)S(1)}, ...), condition=%wide.region_19.20_spmd.clone, body=%wide.region_15.19_spmd.clone.sunk | while | flops 511939840 | bytes 13323013 | solution.py:145
  715.5 33.3 %all-gather.17 = bf16[24,64,64]{2,1,0:T(8,128)(2,1)} all-gather(bf16[3,64,64]{2,1,0:T(8,128)(2,1)S(1)} %convert_element_type.911), channel_id=19, replica_groups=mesh['dp'=8,'head'=4] {'dp'}, dimensions={0}, use_global_device_ids=true | all-gather | bytes 221184 | tf_op jit(solution)/shard_map/all_gather | solution.py:29
  748.9 33.1 %all-gather.16 = bf16[24,64,64]{2,1,0:T(8,128)(2,1)} all-gather(bf16[3,64,64]{2,1,0:T(8,128)(2,1)S(1)} %convert_element_type.910), channel_id=18, replica_groups=mesh['dp'=8,'head'=4] {'dp'}, dimensions={0}, use_global_device_ids=true | all-gather | bytes 221184 | tf_op jit(solution)/shard_map/all_gather | solution.py:29
  856.4 43.9 %all-gather.23 = bf16[4,1,768]{0,1,2:T(2,128)(2,1)S(1)} all-gather(bf16[4,1,96]{0,1,2:T(2,128)(2,1)S(1)} %copy.604), channel_id=25, replica_groups=mesh['dp'=8,'head'=4] {'dp'}, dimensions={2}, use_global_device_ids=true | all-gather | bytes 6912 | tf_op jit(solution)/shard_map/all_gather | solution.py:306
  974.8 34.3 %while.243 = (s32[]{:T(128)}, f32[3,64,64]{2,1,0:T(8,128)S(1)}, f32[3,64,64]{2,1,0:T(8,128)S(1)}, f32[3,64]{1,0:T(4,128)S(1)}, f32[3,64]{1,0:T(4,128)S(1)}, /*in...) while((s32[]{:T(128)}, f32[3,64,64]{2,1,0:T(8,128)S(1)}, ...), condition=%wide.region_36.37_spmd.clone, body=%wide.region_33.36_spmd.clone.sunk | while | flops 151685760 | bytes 2590997 | solution.py:145
  1166.0 175.0 %while.238 = (s32[]{:T(128)}, f32[3,64,64]{2,1,0:T(8,128)S(1)}, f32[3,64,64]{2,1,0:T(8,128)}, f32[3,64]{1,0:T(4,128)}, f32[3,64]{1,0:T(4,128)}, /*index=5*/f32[4...) while((s32[]{:T(128)}, f32[3,64,64]{2,1,0:T(8,128)S(1)}, ...), condition=%wide.region_38.39_spmd, body=%wide.region_37.38_spmd.sunk | while | flops 1120195840 | bytes 35867116 | solution.py:145
  1368.8 45.6 %all-to-all-done.5 = bf16[2048,3,1,192]{3,1,2,0:T(4,128)(2,1)} async-done(((bf16[2048,3,1,192]{3,1,2,0:T(4,128)(2,1)}), bf16[2048,3,1,192]{3,1,2,0:T(4,128)(2,1)}, u32[]{:S(2)}, u32[]{:S(2)}) %all-to-all-start.5) | async-done | bytes 2359328 | tf_op jit(solution)/shard_map/all_to_all | solution.py:425
  1479.1 35.7 %while.245 = (s32[]{:T(128)}, f32[3,64,64]{2,1,0:T(8,128)S(1)}, f32[3,64,64]{2,1,0:T(8,128)S(1)}, f32[3,64]{1,0:T(4,128)S(1)}, f32[3,64]{1,0:T(4,128)S(1)}, /*in...) while((s32[]{:T(128)}, f32[3,64,64]{2,1,0:T(8,128)S(1)}, ...), condition=%wide.region_49.50_spmd.clone, body=%wide.region_46.49_spmd.clone.sunk | while | flops 151685760 | bytes 2493201 | solution.py:145
  1581.6 33.4 %all-gather.33 = bf16[24,64,64]{2,1,0:T(8,128)(2,1)S(1)} all-gather(bf16[3,64,64]{2,1,0:T(8,128)(2,1)S(1)} %fusion.349), channel_id=35, replica_groups=mesh['dp'=8,'head'=4] {'dp'}, dimensions={0}, use_global_device_ids=true | all-gather | bytes 221184 | tf_op jit(solution)/shard_map/all_gather | solution.py:51
  1682.5 170.0 %while.239 = (s32[]{:T(128)}, f32[3,64,64]{2,1,0:T(8,128)S(1)}, f32[3,64,64]{2,1,0:T(8,128)}, f32[3,64]{1,0:T(4,128)}, f32[3,64]{1,0:T(4,128)}, /*index=5*/f32[4...) while((s32[]{:T(128)}, f32[3,64,64]{2,1,0:T(8,128)S(1)}, ...), condition=%wide.region_51.52_spmd, body=%wide.region_50.51_spmd.sunk | while | flops 1120195840 | bytes 35916380 | solution.py:145
  1873.0 54.0 %all_to_all.84 = bf16[2048,3,1,192]{3,1,2,0:T(4,128)(2,1)} all-to-all(bf16[2048,3,1,192]{3,1,2,0:T(4,128)(2,1)} %copy.631), channel_id=1, replica_groups=mesh['dp'=8,'head'=4] {'head'}, dimensions={0} | all-to-all | bytes 4718592 | tf_op jit(solution)/shard_map/all_to_all | solution.py:425
  2014.9 79.7 %reduce-scatter.55.cloned.1.call-done = f32[96,2304]{1,0:T(8,128)} async-done(((f32[768,2304]{1,0:T(8,128)}), f32[96,2304]{1,0:T(8,128)}) %reduce-scatter.55.cloned.1.call-update) | async-done | bytes 884752
  2096.9 163.6 %reduce-scatter.53.cloned.1.call-done = f32[384,768]{1,0:T(8,128)} async-done(((f32[3072,768]{1,0:T(8,128)}), f32[384,768]{1,0:T(8,128)}) %reduce-scatter.53.cloned.1.call-update) | async-done | bytes 1179664 | tf_op jit(solution)/shard_map/reduce_scatter | solution.py:450
  2264.8 161.5 %reduce-scatter.51.cloned.1.call-done = f32[384,768]{1,0:T(8,128)} async-done(((f32[3072,768]{1,0:T(8,128)}), f32[384,768]{1,0:T(8,128)}) %reduce-scatter.51.cloned.1.call-update) | async-done | bytes 1179664 | tf_op jit(solution)/shard_map/reduce_scatter | solution.py:450
  2430.7 161.5 %reduce-scatter.47.cloned.1.call-done = f32[96,3072]{1,0:T(8,128)} async-done(((f32[768,3072]{1,0:T(8,128)}), f32[96,3072]{1,0:T(8,128)}) %reduce-scatter.47.cloned.1.call-update) | async-done | bytes 1179664 | tf_op jit(solution)/shard_map/reduce_scatter | solution.py:449
  2594.5 163.6 %reduce-scatter.43.cloned.1.call-done = f32[96,3072]{1,0:T(8,128)} async-done(((f32[768,3072]{1,0:T(8,128)}), f32[96,3072]{1,0:T(8,128)}) %reduce-scatter.43.cloned.1.call-update) | async-done | bytes 1179664 | tf_op jit(solution)/shard_map/reduce_scatter | solution.py:449
  2773.8 48.5 %reduce-scatter.69.cloned.1.call-done = f32[96,4]{1,0:T(8,128)} async-done(((f32[768,4]{1,0:T(8,128)}), f32[96,4]{1,0:T(8,128)}) %reduce-scatter.69.cloned.1.call-update) | async-done | bytes 1552
  2823.2 63.3 %reduce-scatter.67.cloned.1.call-done = f32[96,4]{1,0:T(8,128)} async-done(((f32[768,4]{1,0:T(8,128)}), f32[96,4]{1,0:T(8,128)}) %reduce-scatter.67.cloned.1.call-update) | async-done | bytes 1552
  3095.2 39.3 %psum.7 = f32[]{:T(128)} all-reduce(f32[]{:T(128)S(6)} %add.757), channel_id=1, replica_groups=mesh['dp'=8,'head'=4] {'dp','head'}, use_global_device_ids=true, to_apply=%region_85.86 | all-reduce | flops 1 | bytes 8 | tf_op jit(solution)/shard_map/psum | solution.py:478
  (1495 shorter events, 1887.4 us)
Async XLA Ops:
  23.6 466.8 %all-gather.55.cloned.1.call-start = ((), (), s32[]{:S(2)}) async-start(), calls=%async_computation.37 | async-start | bytes 1327104 | tf_op jit(solution)/shard_map/all_gather | solution.py:303
  31.5 462.6 %all-gather.57.cloned.1.call-start = ((), (), s32[]{:S(2)}) async-start(), calls=%async_computation.38 | async-start | bytes 5308416 | tf_op jit(solution)/shard_map/all_gather | solution.py:304
  40.4 473.8 %all-gather.59.cloned.1.call-start = ((), (), s32[]{:S(2)}) async-start(), calls=%async_computation.39 | async-start | bytes 5308416 | tf_op jit(solution)/shard_map/all_gather | solution.py:305
  48.6 472.1 %all-gather.61.cloned.1.call-start = ((), (), s32[]{:S(2)}) async-start(), calls=%async_computation.40 | async-start | bytes 3981312 | tf_op jit(solution)/shard_map/all_gather | solution.py:302
  108.2 813.6 %all-gather.63.cloned.1.call-start = ((), (), s32[]{:S(2)}) async-start(), calls=%async_computation.41 | async-start | bytes 1327104 | tf_op jit(solution)/shard_map/all_gather | solution.py:303
  412.9 511.8 %all-gather.65.cloned.1.call-start = ((), (), s32[]{:S(2)}) async-start(), calls=%async_computation.42 | async-start | bytes 5308416 | tf_op jit(solution)/shard_map/all_gather | solution.py:304
  542.6 401.9 %all-gather.67.cloned.1.call-start = ((), (), s32[]{:S(2)}) async-start(), calls=%async_computation.43 | async-start | bytes 5308416 | tf_op jit(solution)/shard_map/all_gather | solution.py:305
  1366.2 642.6 %reduce-scatter.41.cloned.1.call-start = ((), (), s32[]{:S(2)}) async-start(), calls=%async_computation.29 | async-start | bytes 2654208 | tf_op jit(solution)/shard_map/reduce_scatter | solution.py:448
  1472.9 537.7 %reduce-scatter.39.cloned.1.call-start = ((), (), s32[]{:S(2)}) async-start(), calls=%async_computation.28 | async-start | bytes 2654208 | tf_op jit(solution)/shard_map/reduce_scatter | solution.py:448
  1476.9 535.6 %reduce-scatter.57.cloned.1.call-start = ((), (), s32[]{:S(2)}) async-start(), calls=%async_computation.45 | async-start | bytes 7962624
  1526.5 568.1 %reduce-scatter.55.cloned.1.call-start = ((), (), s32[]{:S(2)}) async-start(), calls=%async_computation.44 | async-start | bytes 7962624
  1977.3 449.1 %reduce-scatter.51.cloned.1.call-start = ((), (), s32[]{:S(2)}) async-start(), calls=%async_computation.34 | async-start | bytes 10616832 | tf_op jit(solution)/shard_map/reduce_scatter | solution.py:450
  1986.5 605.7 %reduce-scatter.47.cloned.1.call-start = ((), (), s32[]{:S(2)}) async-start(), calls=%async_computation.32 | async-start | bytes 10616832 | tf_op jit(solution)/shard_map/reduce_scatter | solution.py:449
  1996.2 761.9 %reduce-scatter.43.cloned.1.call-start = ((), (), s32[]{:S(2)}) async-start(), calls=%async_computation.30 | async-start | bytes 10616832 | tf_op jit(solution)/shard_map/reduce_scatter | solution.py:449
  2005.9 816.4 %reduce-scatter.69.cloned.1.call-start = ((), (), s32[]{:S(2)}) async-start(), calls=%async_computation.51 | async-start | bytes 442368
  2007.5 878.9 %reduce-scatter.67.cloned.1.call-start = ((), (), s32[]{:S(2)}) async-start(), calls=%async_computation.50 | async-start | bytes 442368
  2008.7 899.5 %reduce-scatter.61.cloned.1.call-start = ((), (), s32[]{:S(2)}) async-start(), calls=%async_computation.47 | async-start | bytes 245760
  2010.6 920.3 %reduce-scatter.59.cloned.1.call-start = ((), (), s32[]{:S(2)}) async-start(), calls=%async_computation.46 | async-start | bytes 245760
  2012.5 943.5 %reduce-scatter.37.cloned.1.call-start = ((), (), s32[]{:S(2)}) async-start(), calls=%async_computation.27 | async-start | bytes 737280 | tf_op jit(solution)/shard_map/reduce_scatter | solution.py:454
  2014.8 966.4 %reduce-scatter.35.cloned.1.call-start = ((), (), s32[]{:S(2)}) async-start(), calls=%async_computation.26 | async-start | bytes 737280 | tf_op jit(solution)/shard_map/reduce_scatter | solution.py:454
  2096.8 909.5 %reduce-scatter.65.cloned.1.call-start = ((), (), s32[]{:S(2)}) async-start(), calls=%async_computation.49 | async-start | bytes 737280
  2264.8 766.6 %reduce-scatter.63.cloned.1.call-start = ((), (), s32[]{:S(2)}) async-start(), calls=%async_computation.48 | async-start | bytes 737280
  2430.6 625.9 %reduce-scatter.49.cloned.1.call-start = ((), (), s32[]{:S(2)}) async-start(), calls=%async_computation.33 | async-start | bytes 737280 | tf_op jit(solution)/shard_map/reduce_scatter | solution.py:460
  2594.4 487.1 %reduce-scatter.45.cloned.1.call-start = ((), (), s32[]{:S(2)}) async-start(), calls=%async_computation.31 | async-start | bytes 737280 | tf_op jit(solution)/shard_map/reduce_scatter | solution.py:460
  (265 other events, 5163.3 us)
Sparse Core Ops, SparseCore 0:
  23.7 66.0 all-gather.52
  92.6 39.5 all-gather.54
  134.3 79.0 all-gather.56
  215.3 80.1 all-gather.58
  298.0 68.8 all-gather.60
  369.5 39.7 all-gather.62
  429.1 93.0 all-gather.64
  575.7 82.6 all-gather.66
  1370.5 68.1 reduce-scatter.40
  1477.0 68.1 reduce-scatter.38
  1549.0 138.4 reduce-scatter.56
  1968.0 126.5 reduce-scatter.54
  2098.2 162.3 reduce-scatter.52
  2263.9 162.3 reduce-scatter.50
  2429.8 162.3 reduce-scatter.46
  2595.7 162.3 reduce-scatter.42
  2761.8 60.4 reduce-scatter.68
  2826.0 60.3 reduce-scatter.66
  2933.9 22.0 reduce-scatter.36
  2959.1 22.0 reduce-scatter.34
  2984.2 22.0 reduce-scatter.64
  3009.3 22.0 reduce-scatter.62
  3034.4 22.0 reduce-scatter.48
  3059.4 22.0 reduce-scatter.44
  (2 shorter events, 38.3 us)
where the time goes:
time: 3180 us; the launch traced here: 3160 us
  waiting for transfers between devices  1090 us (34%)
  blocking collectives  746 us (23%)
  local copies, waits for them, and re-layouts  571 us (18%)
  matrix products  454 us (14%)
  other arithmetic  191 us (6%)
  loops' own time  47.2 us (1%)
    reduce_scatter x2, waiting for transfers between devices, body(): lax.psum_scatter(grad_set[2], 'dp', scatter_dimension=0, tiled=True)  325 us
    reduce_scatter x2, waiting for transfers between devices, body(): lax.psum_scatter(grad_set[3], 'dp', scatter_dimension=0, tiled=True)  325 us
    unnamed x34, waiting for transfers between devices  273 us
    dynamic_update_slice x56, local copies, waits for them, and re-layouts, run_blocks(): lax.scan(jax.checkpoint(block_step), initial, (by_blocks(queries), by_blo...  213 us
    all_gather x8, blocking collectives, carried_in(): lax.all_gather(a.astype(kind), axis)  203 us
    all_gather x8, blocking collectives, carried_in_2(): lax.all_gather(part.astype(kind), axis)  200 us
    unnamed x391, local copies, waits for them, and re-layouts  86 us
    all_gather x2, blocking collectives, body(): lax.all_gather(shards[4], 'dp', axis=1, tiled=True)  85.3 us
  transfers between devices with their start and end apart: 33, of which 17 were waited for; matrix products, arithmetic and copies ran while one was open for 29% of the time, Pallas kernels for 0%

commit v1 on v0

v1 whole, which is shorter than its diff:
```python
import functools
import math
import jax
import jax.numpy as jnp
from jax import lax
from jax.experimental import pallas as pl
from jax.experimental.pallas import tpu as pltpu
from jax.sharding import PartitionSpec as P

HEADS = 12
LONGEST = 8192

exact_mode = lax.Precision.HIGHEST
beta_one = 0.9
beta_two = 0.999
adam_eps = 1e-08
decay_rate = 0.1
rate_matrix = 0.1
rate_outproj = 0.5
rate_norm = 0.5
clip_limit = 1.0
norm_eps = 1e-05
step_fixed = 10.0

MESH = pl.DeviceIdType.MESH


def place():
    dp, hd = lax.axis_index("dp"), lax.axis_index("head")
    return dp // 2, dp % 2, hd // 2, hd % 2


def at(z, x, y, c):
    return (z * 2 + x, y * 2 + c)


def greet(partners):
    barrier = pltpu.get_barrier_semaphore()
    for dev in partners:
        pl.semaphore_signal(barrier, inc=1, device_id=dev, device_id_type=MESH)
    pl.semaphore_wait(barrier, len(partners))


def gather_kernel(dims, *refs):
    count = len(dims)
    pieces, fulls = refs[:count], refs[count : 2 * count]
    send_sem, recv_sem, own_sem = refs[2 * count :]
    z, x, y, c = place()
    nx, ny, nc = 1 - x, 1 - y, 1 - c
    zs = [z] + [(z + d) % 4 for d in (1, 2, 3)]
    zo = [z] + [(z + 4 - d) % 4 for d in (1, 2, 3)]
    greet(
        [at(zs[d], x, y, c) for d in (1, 2, 3)]
        + [at(z, nx, y, c), at(z, x, ny, c), at(z, x, y, nc)]
    )

    def spot(t, zz, xx, yy):
        rows, cols, flat = dims[t]
        if flat:
            first = (((zz * 2 + xx) * 2 + yy) * 2 + c) * rows
            left = 0
        else:
            first = ((zz * 2 + xx) * 2 + c) * rows
            left = yy * cols
        return fulls[t].at[
            :, pl.ds(pl.multiple_of(first, rows), rows), pl.ds(pl.multiple_of(left, cols), cols)
        ]

    sent = {}

    def send(t, key, src, dst, dev):
        k = KEYS[key]
        copy = pltpu.make_async_remote_copy(
            src_ref=src,
            dst_ref=dst,
            send_sem=send_sem.at[t, k],
            recv_sem=recv_sem.at[t, k],
            device_id=dev,
            device_id_type=MESH,
        )
        copy.start()
        sent[t, key] = copy

    def forward(t, key, zz, xx, yy, dev):
        block = spot(t, zz, xx, yy)
        send(t, key, block, block, dev)

    to_x, to_y, to_c = at(z, nx, y, c), at(z, x, ny, c), at(z, x, y, nc)

    def fan(t, d):
        src = pieces[t] if d == 0 else spot(t, zo[d], x, y)
        dst = spot(t, zo[d], x, y)
        send(t, ("x", d), src, dst, to_x)
        send(t, ("y", d), src, dst, to_y)
        send(t, ("c", d), src, dst, to_c)

    def second(t, d):
        sent[t, ("x", d)].wait_recv()
        if d in FIRST_X:
            forward(t, ("d", d), zo[d], nx, y, to_y)
        forward(t, ("cx", d), zo[d], nx, y, to_c)
        sent[t, ("y", d)].wait_recv()
        if d not in FIRST_X:
            forward(t, ("d", d), zo[d], x, ny, to_x)
        forward(t, ("cy", d), zo[d], x, ny, to_c)

    def third(t, d):
        sent[t, ("d", d)].wait_recv()
        forward(t, ("cd", d), zo[d], nx, ny, to_c)

    owns = []
    for t in range(count):
        for d in (1, 2, 3):
            send(t, ("z", d), pieces[t], spot(t, z, x, y), at(zs[d], x, y, c))
        fan(t, 0)
        own = pltpu.make_async_copy(pieces[t], spot(t, z, x, y), own_sem.at[t])
        own.start()
        owns.append(own)
    for step in range(count + 2):
        for d in (1, 3, 2):
            if step < count:
                sent[step, ("z", d)].wait_recv()
                fan(step, d)
        for d in (0, 1, 3, 2):
            if 0 <= step - 1 < count:
                second(step - 1, d)
        for d in (0, 1, 3, 2):
            if 0 <= step - 2 < count:
                third(step - 2, d)
    for t in range(count):
        for kind in ("c", "cx", "cy", "cd"):
            for d in range(4):
                sent[t, (kind, d)].wait_recv()
    for copy in sent.values():
        copy.wait_send()
    for own in owns:
        own.wait()


FIRST_X = (0, 3)
KEYS = {("z", d): d - 1 for d in (1, 2, 3)}
for kind in ("x", "y", "c", "d", "cx", "cy", "cd"):
    for d in range(4):
        KEYS[kind, d] = len(KEYS)


def gather_all(pieces, flats, layers):
    dims = tuple((p.shape[1], p.shape[2], f) for p, f in zip(pieces, flats))
    shapes = [
        jax.ShapeDtypeStruct(
            (p.shape[0], p.shape[1] * 32, p.shape[2])
            if f
            else (p.shape[0], p.shape[1] * 16, p.shape[2] * 2),
            p.dtype,
        )
        for p, f in zip(pieces, flats)
    ]
    count = len(pieces)
    anywhere = pl.BlockSpec(memory_space=pl.ANY)
    return pl.pallas_call(
        functools.partial(gather_kernel, dims),
        out_shape=shapes,
        in_specs=[anywhere] * count,
        out_specs=[anywhere] * count,
        scratch_shapes=[
            pltpu.SemaphoreType.DMA((count, len(KEYS))),
            pltpu.SemaphoreType.DMA((count, len(KEYS))),
            pltpu.SemaphoreType.DMA((count,)),
        ],
        compiler_params=pltpu.CompilerParams(collective_id=0, has_side_effects=True),
        name="gather_weights",
    )(*pieces)

RS_KEYS = {"core": 0}
for stage in ("one", "two"):
    for d in range(4):
        RS_KEYS[stage, d] = len(RS_KEYS)
for d in (1, 2, 3):
    RS_KEYS["z", d] = len(RS_KEYS)


def reduce_kernel(dims, *refs):
    count = len(dims)
    grads, outs, total_out = refs[:count], refs[count : 2 * count], refs[2 * count]
    rest = refs[2 * count + 1 :]
    own, from_core, one_y, one_x, two, from_z = (
        rest[i * count : (i + 1) * count] for i in range(6)
    )
    square, sq_plane, sq_z, send_sem, recv_sem, own_sem, sq_send, sq_recv = rest[6 * count :]
    z, x, y, c = place()
    nx, ny, nc = 1 - x, 1 - y, 1 - c
    zs = [z] + [(z + d) % 4 for d in (1, 2, 3)]
    to_x, to_y, to_c = at(z, nx, y, c), at(z, x, ny, c), at(z, x, y, nc)
    plane = plane_partners(z, x, y, c)
    greet([at(zs[d], x, y, c) for d in (1, 2, 3)] + plane)
    sent = {}

    def send(t, key, src, dst, dev):
        k = RS_KEYS[key]
        copy = pltpu.make_async_remote_copy(
            src_ref=src,
            dst_ref=dst,
            send_sem=send_sem.at[t, k],
            recv_sem=recv_sem.at[t, k],
            device_id=dev,
            device_id_type=MESH,
        )
        copy.start()
        sent[t, key] = copy

    owns = []
    for t in range(count):
        send(t, "core", grads[t].at[:, nc], from_core[t], to_c)
        copy = pltpu.make_async_copy(grads[t].at[:, c], own[t], own_sem.at[t])
        copy.start()
        owns.append(copy)

    def cols(t, yy):
        width = dims[t][1]
        return pl.ds(pl.multiple_of(yy * width, width), width)

    def add(ref, other):
        ref[...] = (ref[...].astype(jnp.float32) + other.astype(jnp.float32)).astype(ref.dtype)

    def stage_one(t):
        owns[t].wait()
        sent[t, "core"].wait_recv()
        for d in (2, 3, 1, 0):
            strip = own[t].at[pl.ds(zs[d] * 2, 2)]
            add(strip, from_core[t][pl.ds(zs[d] * 2, 2)])
            if d in FIRST_X:
                send(t, ("one", d), strip.at[:, :, cols(t, ny)], one_y[t].at[FIRST_X.index(d)], to_y)
            else:
                send(t, ("one", d), strip.at[nx], one_x[t].at[d - 1], to_x)

    def stage_two(t):
        for d in (2, 3, 1, 0):
            sent[t, ("one", d)].wait_recv()
            sent[t, ("one", d)].wait_send()
            strip = own[t].at[pl.ds(zs[d] * 2, 2)]
            if d in FIRST_X:
                add(strip.at[:, :, cols(t, y)], one_y[t][FIRST_X.index(d)])
                send(t, ("two", d), strip.at[nx, :, cols(t, y)], two[t].at[d], to_x)
            else:
                add(strip.at[x], one_x[t][d - 1])
                send(t, ("two", d), strip.at[x, :, cols(t, ny)], two[t].at[d], to_y)

    def stage_three(t):
        for d in (2, 3, 1, 0):
            sent[t, ("two", d)].wait_recv()
            block = own[t].at[zs[d] * 2 + x, :, cols(t, y)]
            add(block, two[t][d])
            if d > 0:
                send(t, ("z", d), block, from_z[t].at[d - 1], at(zs[d], x, y, c))

    def stage_four(t):
        value = own[t][z * 2 + x, :, cols(t, y)].astype(jnp.float32)
        for d in (1, 2, 3):
            sent[t, ("z", d)].wait_recv()
            value = value + from_z[t][d - 1].astype(jnp.float32)
        outs[t][...] = value
        squares = value * value
        rows, width = dims[t]
        part = jnp.sum(squares.reshape(rows // 8, 8, width), axis=0)
        folded = part[:, :128]
        for j in range(1, width // 128):
            folded = folded + part[:, j * 128 : (j + 1) * 128]
        return folded

    total = jnp.zeros((8, 128), jnp.float32)
    for step in range(count + 3):
        if step < count:
            stage_one(step)
        if 0 <= step - 1 < count:
            stage_two(step - 1)
        if 0 <= step - 2 < count:
            stage_three(step - 2)
        if 0 <= step - 3 < count:
            total = total + stage_four(step - 3)
    square[0] = total
    copies = []
    for d in (1, 2, 3):
        copy = pltpu.make_async_remote_copy(
            src_ref=square.at[0],
            dst_ref=sq_z.at[d - 1],
            send_sem=sq_send.at[d - 1],
            recv_sem=sq_recv.at[d - 1],
            device_id=at(zs[d], x, y, c),
            device_id_type=MESH,
        )
        copy.start()
        copies.append(copy)
    for d in (1, 2, 3):
        copies[d - 1].wait_recv()
        total = total + sq_z[d - 1]
    square[1] = total
    for j, dev in enumerate(plane):
        copy = pltpu.make_async_remote_copy(
            src_ref=square.at[1],
            dst_ref=sq_plane.at[j],
            send_sem=sq_send.at[3 + j],
            recv_sem=sq_recv.at[3 + j],
            device_id=dev,
            device_id_type=MESH,
        )
        copy.start()
        copies.append(copy)
    for j in range(len(plane)):
        copies[3 + j].wait_recv()
        total = total + sq_plane[j]
    total_out[...] = total
    for (t, key), copy in sent.items():
        if not (isinstance(key, tuple) and key[0] == "one"):
            copy.wait_send()
    for copy in copies:
        copy.wait_send()


def plane_partners(z, x, y, c):
    out = []
    for d in range(1, 8):
        dx, dy, dc = d // 4, (d // 2) % 2, d % 2
        out.append(at(z, 1 - x if dx else x, 1 - y if dy else y, 1 - c if dc else c))
    return out


def reduce_all(grads):
    dims = tuple((g.shape[2], g.shape[3] // 2) for g in grads)
    count = len(grads)
    kind = grads[0].dtype
    vm = lambda *s: pltpu.VMEM(s, kind)
    scratch = (
        [vm(8, r, 2 * w) for r, w in dims]
        + [vm(8, r, 2 * w) for r, w in dims]
        + [vm(2, 2, r, w) for r, w in dims]
        + [vm(2, r, 2 * w) for r, w in dims]
        + [vm(4, r, w) for r, w in dims]
        + [vm(3, r, w) for r, w in dims]
        + [
            pltpu.VMEM((2, 8, 128), jnp.float32),
            pltpu.VMEM((7, 8, 128), jnp.float32),
            pltpu.VMEM((3, 8, 128), jnp.float32),
            pltpu.SemaphoreType.DMA((count, len(RS_KEYS))),
            pltpu.SemaphoreType.DMA((count, len(RS_KEYS))),
            pltpu.SemaphoreType.DMA((count,)),
            pltpu.SemaphoreType.DMA((10,)),
            pltpu.SemaphoreType.DMA((10,)),
        ]
    )
    return pl.pallas_call(
        functools.partial(reduce_kernel, dims),
        out_shape=[jax.ShapeDtypeStruct((r, w), jnp.float32) for r, w in dims]
        + [jax.ShapeDtypeStruct((8, 128), jnp.float32)],
        in_specs=[pl.BlockSpec(memory_space=pl.ANY)] * count,
        out_specs=[pl.BlockSpec(memory_space=pltpu.VMEM)] * (count + 1),
        scratch_shapes=scratch,
        compiler_params=pltpu.CompilerParams(
            collective_id=1, has_side_effects=True, vmem_limit_bytes=60 * 2**20
        ),
        name="reduce_gradients",
    )(*grads)

HD = 64


def flip(z, x, y, c, d):
    dx, dy, dc = d // 4, (d // 2) % 2, d % 2
    return 1 - x if dx else x, 1 - y if dy else y, 1 - c if dc else c


class Exchange:
    def __init__(self, coef, send_all, got, sums, got_z, back, result, sems, reverse):
        self.coef, self.reverse = coef, reverse
        self.mine, self.got, self.sums = send_all, got, sums
        self.got_z, self.back, self.result = got_z, back, result
        self.sems = sems
        self.z, self.x, self.y, self.c = place()
        self.index = self.x * 4 + self.y * 2 + self.c
        self.copies = []

    def partners(self):
        z, x, y, c = self.z, self.x, self.y, self.c
        return [at((z + d) % 4, x, y, c) for d in (1, 2, 3)] + plane_partners(z, x, y, c)

    def send(self, k, src, dst, dev):
        copy = pltpu.make_async_remote_copy(
            src_ref=src,
            dst_ref=dst,
            send_sem=self.sems[0].at[k],
            recv_sem=self.sems[1].at[k],
            device_id=dev,
            device_id_type=MESH,
        )
        copy.start()
        self.copies.append(copy)

    def scatter(self):
        self.got[self.index] = self.mine[self.index]
        for d in range(1, 8):
            nx, ny, nc = flip(self.z, self.x, self.y, self.c, d)
            self.send(
                d - 1,
                self.mine.at[nx * 4 + ny * 2 + nc],
                self.got.at[self.index],
                at(self.z, nx, ny, nc),
            )

    def across(self):
        for k in range(7):
            self.copies[k].wait_recv()
        for d in (1, 2, 3):
            other = (self.z + d) % 4
            total = jnp.zeros(self.got.shape[1:], jnp.float32)
            for j in range(8):
                total = total + self.coef[8 + d, j] * self.got[j].astype(jnp.float32)
            self.sums[d - 1] = total.astype(jnp.bfloat16)
            self.send(
                6 + d,
                self.sums.at[d - 1],
                self.got_z.at[d - 1],
                at(other, self.x, self.y, self.c),
            )

    def gather(self):
        for k in (7, 8, 9):
            self.copies[k].wait_recv()
        parts = [self.got[j].astype(jnp.float32) for j in range(8)]
        parts += [self.got_z[d].astype(jnp.float32) for d in range(3)]
        for i in range(8):
            total = jnp.zeros(self.got.shape[1:], jnp.float32)
            span = range(i + 1, 8) if self.reverse else range(i)
            for j in list(span) + [8, 9, 10]:
                total = total + self.coef[i, j] * parts[j]
            self.back[i] = total.astype(jnp.bfloat16)
        self.result[self.index] = self.back[self.index]
        for d in range(1, 8):
            nx, ny, nc = flip(self.z, self.x, self.y, self.c, d)
            self.send(
                9 + d,
                self.back.at[nx * 4 + ny * 2 + nc],
                self.result.at[self.index],
                at(self.z, nx, ny, nc),
            )

    def finish(self):
        for k in range(10, 17):
            self.copies[k].wait_recv()
        for copy in self.copies:
            copy.wait_send()


def exchange_scratch(width):
    return [
        pltpu.VMEM((8, 16, width), jnp.bfloat16),
        pltpu.VMEM((8, 16, width), jnp.bfloat16),
        pltpu.VMEM((3, 16, width), jnp.bfloat16),
        pltpu.VMEM((3, 16, width), jnp.bfloat16),
        pltpu.VMEM((8, 16, width), jnp.bfloat16),
        pltpu.VMEM((8, 16, width), jnp.bfloat16),
        pltpu.SemaphoreType.DMA((17,)),
        pltpu.SemaphoreType.DMA((17,)),
    ]


def mm(a, b):
    return lax.dot_general(a, b, (((1,), (0,)), ((), ())), preferred_element_type=jnp.float32)


def mm_nt(a, b):
    return lax.dot_general(a, b, (((1,), (1,)), ((), ())), preferred_element_type=jnp.float32)


def low_lanes(shape):
    return lax.broadcasted_iota(jnp.int32, shape, len(shape) - 1) < HD


def lane_is(shape, h):
    return lax.broadcasted_iota(jnp.int32, shape, len(shape) - 1) == h


def pair_cols(p):
    return slice(p * 128, (p + 1) * 128)


def pack_state(ref, p, kind, block, extra):
    first = kind * 64
    low = low_lanes((64, 128))
    packed = jnp.where(low, block[:64, :128], block[64:, :128]).astype(jnp.bfloat16)
    for s in range(4):
        ref[kind * 4 + s, :, pair_cols(p)] = packed[s * 16 : (s + 1) * 16]
    if extra is None:
        extra = jnp.zeros((64, 128), jnp.float32)
    extra = extra + jnp.where(lane_is((64, 128), 2 * p), block[:64, 128:], 0.0)
    return extra + jnp.where(lane_is((64, 128), 2 * p + 1), block[64:, 128:], 0.0)


def store_extra(ref, kind, extra, width):
    extra = extra.astype(jnp.bfloat16)
    for s in range(4):
        ref[kind * 4 + s, :, width - 128 :] = extra[s * 16 : (s + 1) * 16]


def unpack_state(ref, p, kind, width):
    packed = jnp.concatenate([ref[kind * 4 + s, :, pair_cols(p)] for s in range(4)], axis=0)
    sums = jnp.concatenate([ref[kind * 4 + s, :, width - 128 :] for s in range(4)], axis=0)
    low = low_lanes((64, 128))
    zero = jnp.zeros((64, 128), jnp.bfloat16)
    top = jnp.concatenate(
        [jnp.where(low, packed, zero), jnp.where(lane_is((64, 128), 2 * p), sums, zero)], axis=1
    )
    bottom = jnp.concatenate(
        [jnp.where(low, zero, packed), jnp.where(lane_is((64, 128), 2 * p + 1), sums, zero)],
        axis=1,
    )
    return jnp.concatenate([top, bottom], axis=0)


def spread(values, p):
    rows = values.shape[0]
    first = jnp.broadcast_to(values[:, 2 * p : 2 * p + 1], (rows, 128))
    second = jnp.broadcast_to(values[:, 2 * p + 1 : 2 * p + 2], (rows, 128))
    return jnp.where(low_lanes((rows, 128)), first, second)


def attend_kernel(pairs, coef, q_ref, k_ref, v_ref, w_ref, aux_ref, ob_ref, den_ref, state_ref, num, *rest):
    rows = q_ref.shape[0]
    half = rows // 2
    width = pairs * 128 + 128
    ex = Exchange(coef, *rest[:6], rest[6:8], False)
    greet(ex.partners())
    cos, sin = aux_ref[:, 0:1], aux_ref[:, 1:2]
    follow, tail = aux_ref[:, 2:3], aux_ref[:, 3:4]
    ones = jnp.ones((rows, 128), jnp.bfloat16)
    extras = [None, None]
    for p in range(pairs):
        kp = k_ref[:, pair_cols(p)].astype(jnp.float32) * tail
        rhs = jnp.concatenate([v_ref[:, pair_cols(p)], ones], axis=1)
        for kind, angle in enumerate((cos, sin)):
            block = mm((kp * angle).T.astype(jnp.bfloat16), rhs)
            extras[kind] = pack_state(ex.mine, p, kind, block, extras[kind])
    for kind in range(2):
        store_extra(ex.mine, kind, extras[kind], width)
    ex.scatter()

    def inner(p):
        kp = k_ref[:, pair_cols(p)]
        vp = v_ref[:, pair_cols(p)]
        low = low_lanes((rows, 128))
        zero = jnp.zeros((rows, 128), jnp.bfloat16)
        parts = []
        for e in range(2):
            h = 2 * p + e
            qh = jnp.where(low if e == 0 else ~low, q_ref[:, pair_cols(p)], zero)
            rhs = jnp.concatenate([vp, lane_is((rows, 128), h).astype(jnp.bfloat16)], axis=1)
            top = (mm_nt(qh[:half], kp[:half]) * w_ref[:half, :half]).astype(jnp.bfloat16)
            bottom = (mm_nt(qh[half:], kp) * w_ref[half:, :]).astype(jnp.bfloat16)
            parts.append(jnp.concatenate([mm(top, rhs[:half]), mm(bottom, rhs)], axis=0))
        num[:, pair_cols(p)] = jnp.where(low, parts[0][:, :128], parts[1][:, :128])
        dens = parts[0][:, 128:] + parts[1][:, 128:]
        if p == 0:
            den_ref[...] = dens
        else:
            den_ref[...] += dens

    third = max(1, pairs // 3)
    for p in range(third):
        inner(p)
    ex.across()
    for p in range(third, 2 * third):
        inner(p)
    ex.gather()
    for p in range(2 * third, pairs):
        inner(p)
    ex.finish()
    state_ref[...] = ex.result[...]
    den = den_ref[...]
    cf, sf = cos * follow, sin * follow
    for p in range(pairs):
        qp = q_ref[:, pair_cols(p)]
        extra = cf * mm(qp, unpack_state(ex.result, p, 0, width))
        extra += sf * mm(qp, unpack_state(ex.result, p, 1, width))
        num[:, pair_cols(p)] += extra[:, :128]
        den = den + extra[:, 128:]
    den_ref[...] = den
    inv = 1.0 / jnp.maximum(den, 1.0)
    for p in range(pairs):
        ob_ref[:, pair_cols(p)] = (num[:, pair_cols(p)] * spread(inv, p)).astype(jnp.bfloat16)


def attend(q, k, v, w, aux, coef):
    rows, model = q.shape
    pairs = model // 128
    width = model + 128
    vmem = pl.BlockSpec(memory_space=pltpu.VMEM)
    return pl.pallas_call(
        functools.partial(attend_kernel, pairs),
        out_shape=[
            jax.ShapeDtypeStruct((rows, model), jnp.bfloat16),
            jax.ShapeDtypeStruct((rows, 128), jnp.float32),
            jax.ShapeDtypeStruct((8, 16, width), jnp.bfloat16),
        ],
        in_specs=[pl.BlockSpec(memory_space=pltpu.SMEM)] + [vmem] * 5,
        out_specs=[vmem] * 3,
        scratch_shapes=[pltpu.VMEM((rows, model), jnp.float32)] + exchange_scratch(width),
        compiler_params=pltpu.CompilerParams(
            collective_id=2, has_side_effects=True, vmem_limit_bytes=48 * 2**20
        ),
        name="attend",
    )(coef, q, k, v, w, aux)


def attend_back_kernel(
    pairs, coef, q_ref, k_ref, v_ref, dob_ref, ob_ref, den_ref, state_ref, w_ref, aux_ref,
    out_ref, dn_ref, dd_ref, *rest,
):
    rows = q_ref.shape[0]
    half = rows // 2
    model = pairs * 128
    width = model + 128
    ex = Exchange(coef, *rest[:6], rest[6:8], True)
    greet(ex.partners())
    cos, sin = aux_ref[:, 0:1], aux_ref[:, 1:2]
    follow, tail = aux_ref[:, 2:3], aux_ref[:, 3:4]
    low = low_lanes((rows, 128))
    zero = jnp.zeros((rows, 128), jnp.bfloat16)
    den = den_ref[...]
    inv = 1.0 / jnp.maximum(den, 1.0)
    dots = jnp.zeros((rows, 128), jnp.float32)
    for p in range(pairs):
        dob = dob_ref[:, pair_cols(p)].astype(jnp.float32)
        dn_ref[:, pair_cols(p)] = (dob * spread(inv, p)).astype(jnp.bfloat16)
        both = dob * ob_ref[:, pair_cols(p)].astype(jnp.float32)
        first = jnp.sum(jnp.where(low, both, 0.0), axis=1, keepdims=True)
        second = jnp.sum(jnp.where(low, 0.0, both), axis=1, keepdims=True)
        dots = dots + jnp.where(lane_is((rows, 128), 2 * p), first, 0.0)
        dots = dots + jnp.where(lane_is((rows, 128), 2 * p + 1), second, 0.0)
    dden = jnp.where(den > 1.0, -dots * inv, 0.0)
    dd_ref[...] = dden
    dden_low = dden.astype(jnp.bfloat16)
    cf, sf = cos * follow, sin * follow
    extras = [None, None]
    for p in range(pairs):
        qp = q_ref[:, pair_cols(p)].astype(jnp.float32)
        rhs = jnp.concatenate([dn_ref[:, pair_cols(p)], dden_low], axis=1)
        for kind, angle in enumerate((cf, sf)):
            block = mm((qp * angle).T.astype(jnp.bfloat16), rhs)
            extras[kind] = pack_state(ex.mine, p, kind, block, extras[kind])
    for kind in range(2):
        store_extra(ex.mine, kind, extras[kind], width)
    ex.scatter()

    def inner(p):
        qp, kp, vp = q_ref[:, pair_cols(p)], k_ref[:, pair_cols(p)], v_ref[:, pair_cols(p)]
        dob = dob_ref[:, pair_cols(p)]
        dnp = dn_ref[:, pair_cols(p)]
        q_t = qp.astype(jnp.float32).T.astype(jnp.bfloat16)
        dn_t = dnp.astype(jnp.float32).T.astype(jnp.bfloat16)
        dq_parts, dk_parts, dv_parts = [], [], []
        for e in range(2):
            h = 2 * p + e
            mask = low if e == 0 else ~low
            span = slice(e * HD, (e + 1) * HD)
            qh = jnp.where(mask, qp, zero)
            doh = jnp.where(mask, dob, zero)
            scale, shift = inv[:, h : h + 1], dd_ref[:, h : h + 1]

            def tile(at_rows, at_cols):
                weight = w_ref[at_rows, at_cols]
                s = (mm_nt(qh[at_rows], kp[at_cols]) * weight).astype(jnp.bfloat16)
                t = mm_nt(doh[at_rows], vp[at_cols])
                ds = (t * scale[at_rows] + shift[at_rows]).astype(jnp.bfloat16)
                g = (ds.astype(jnp.float32) * weight).astype(jnp.bfloat16)
                return s, g

            up, down, every = slice(0, half), slice(half, rows), slice(0, rows)
            s_top, g_top = tile(up, up)
            s_low, g_low = tile(down, every)
            dq_parts.append(jnp.concatenate([mm(g_top, kp[:half]), mm(g_low, kp)], axis=0))

            def turned(left, top, bottom):
                whole = mm(left[span, half:], bottom)
                first = whole[:, :half] + mm(left[span, :half], top)
                return jnp.concatenate([first, whole[:, half:]], axis=1)

            dk_parts.append(turned(q_t, g_top, g_low))
            dv_parts.append(turned(dn_t, s_top, s_low))
        base = p * 128
        dq = jnp.where(low, dq_parts[0], dq_parts[1])
        right = jnp.concatenate([dnp, dden_low], axis=1)
        dq += cf * mm_nt(right, unpack_state(state_ref, p, 0, width))
        dq += sf * mm_nt(right, unpack_state(state_ref, p, 1, width))
        out_ref[:, base : base + 128] = dq.astype(jnp.bfloat16)
        keep[0][:, base : base + 128] = jnp.concatenate(dk_parts, axis=0).T
        keep[1][:, base : base + 128] = jnp.concatenate(dv_parts, axis=0).T

    keep = rest[8:10]
    dden_low = dd_ref[...].astype(jnp.bfloat16)
    third = max(1, pairs // 3)
    for p in range(third):
        inner(p)
    ex.across()
    for p in range(third, 2 * third):
        inner(p)
    ex.gather()
    for p in range(2 * third, pairs):
        inner(p)
    ex.finish()
    ct, st, valid = cos * tail, sin * tail, aux_ref[:, 4:5]
    ones = jnp.ones((rows, 128), jnp.bfloat16)
    for p in range(pairs):
        base = p * 128
        dsc, dss = unpack_state(ex.result, p, 0, width), unpack_state(ex.result, p, 1, width)
        right = jnp.concatenate([v_ref[:, pair_cols(p)], ones], axis=1)
        dk = keep[0][:, base : base + 128] + ct * mm_nt(right, dsc) + st * mm_nt(right, dss)
        kp = k_ref[:, pair_cols(p)]
        dv = keep[1][:, base : base + 128] + ct * mm(kp, dsc[:, :128]) + st * mm(kp, dss[:, :128])
        out_ref[:, model + base : model + base + 128] = (dk * valid).astype(jnp.bfloat16)
        out_ref[:, 2 * model + base : 2 * model + base + 128] = dv.astype(jnp.bfloat16)


def attend_back(q, k, v, dob, ob, den, state, w, aux, coef):
    rows, model = q.shape
    pairs = model // 128
    width = model + 128
    vmem = pl.BlockSpec(memory_space=pltpu.VMEM)
    return pl.pallas_call(
        functools.partial(attend_back_kernel, pairs),
        out_shape=jax.ShapeDtypeStruct((rows, 3 * model), jnp.bfloat16),
        in_specs=[pl.BlockSpec(memory_space=pltpu.SMEM)] + [vmem] * 9,
        out_specs=vmem,
        scratch_shapes=[
            pltpu.VMEM((rows, model), jnp.bfloat16),
            pltpu.VMEM((rows, 128), jnp.float32),
        ]
        + exchange_scratch(width)
        + [pltpu.VMEM((rows, model), jnp.float32)] * 2,
        compiler_params=pltpu.CompilerParams(
            collective_id=3, has_side_effects=True, vmem_limit_bytes=48 * 2**20
        ),
        name="attend_back",
    )(coef, q, k, v, dob, ob, den, state, w, aux)


def stream_meta(lengths, row_ids):
    seq_count = lengths.shape[0]
    seq_ends = jnp.cumsum(lengths, dtype=jnp.int32)
    seq_starts = seq_ends - lengths
    begun = seq_starts[None, :] <= row_ids[:, None]
    seg_raw = jnp.sum(begun.astype(jnp.int32), axis=1, dtype=jnp.int32) - 1
    seg_start = jnp.max(jnp.where(begun, seq_starts[None, :], 0), axis=1)
    inside = row_ids < seq_ends[seq_count - 1]
    seg_ids = jnp.where(inside, seg_raw, seq_count)
    offsets = jnp.where(inside, row_ids - seg_start, 0).astype(jnp.float32)
    angles = offsets * (0.5 * math.pi / LONGEST)
    return (seg_ids, jnp.cos(angles), jnp.sin(angles), inside.astype(jnp.float32))


def layer_norm(inputs_row, gain_row, shift_row):
    mean_row = jnp.mean(inputs_row, axis=-1, keepdims=True)
    centered = inputs_row - mean_row
    variance = jnp.mean(centered * centered, axis=-1, keepdims=True)
    return centered * lax.rsqrt(variance + norm_eps) * gain_row + shift_row


def gelu_exact(inner_pre):
    return jax.nn.gelu(inner_pre, approximate=False)


def contract_rows(left, right):
    return lax.dot_general(
        left, right, (((0,), (0,)), ((), ())), preferred_element_type=jnp.float32
    )


def contract_cols(left, right):
    return lax.dot_general(
        left, right, (((1,), (1,)), ((), ())), preferred_element_type=jnp.float32
    )


def adam_step(weight, first_old, second_old, gradient, factor, step_rate, decay_coef):
    clipped = gradient * factor
    first_new = beta_one * first_old + (1.0 - beta_one) * clipped
    second_new = beta_two * second_old + (1.0 - beta_two) * clipped * clipped
    first_hat = first_new / (1.0 - beta_one**step_fixed)
    second_hat = second_new / (1.0 - beta_two**step_fixed)
    weight_new = weight - step_rate * (
        first_hat / (jnp.sqrt(second_hat) + adam_eps) + decay_coef * weight
    )
    return (weight_new, first_new, second_new)


def other_core(array):
    return lax.ppermute(array, "head", [(0, 1), (1, 0), (2, 3), (3, 2)])


def gather_plan(w_qkv, w_out, w_up, w_down, norm_params):
    first = lax.axis_index("head") % 2 == 0
    low = [a.astype(jnp.bfloat16) for a in (w_qkv, w_out, w_up, w_down)]
    halves = [(a[:, : a.shape[1] // 2], a[:, a.shape[1] // 2 :]) for a in low]
    keep = [jnp.where(first, a, b) for a, b in halves]
    give = [jnp.where(first, b, a) for a, b in halves]
    wide = other_core(jnp.concatenate(give[:3], axis=2))
    got = jnp.split(wide, (keep[0].shape[2], keep[0].shape[2] + keep[1].shape[2]), axis=2)
    got.append(other_core(give[3]))
    pieces = [
        jnp.where(first, jnp.concatenate([a, b], axis=2), jnp.concatenate([b, a], axis=2))
        for a, b in zip(keep, got)
    ]
    layers, _, part = norm_params.shape
    pieces.append(
        jnp.pad(
            norm_params.astype(jnp.bfloat16).reshape(1, layers, part),
            ((0, 0), (0, 16 - layers), (0, 128 - part)),
        )
    )
    fulls = gather_all(pieces, [False] * 5, layers)
    norm = fulls[4].reshape(8, 2, 16, 2, 128)[:, :, :layers, :, :part]
    norm = norm.transpose(2, 3, 1, 0, 4).reshape(layers, 4, 8 * part)
    return fulls[:4], norm


def reduce_plan(grads, norm_grad):
    first = lax.axis_index("head") % 2 == 0
    layers = len(grads)
    flat = []
    for layer in range(layers):
        for g in grads[layer]:
            flat.append(g.reshape(8, 2, g.shape[0] // 16, g.shape[1]))
    part = norm_grad.shape[2] // 8
    norm = norm_grad.astype(jnp.bfloat16).reshape(layers, 2, 2, 8, part).transpose(3, 2, 0, 1, 4)
    norm = jnp.pad(norm, ((0, 0), (0, 0), (0, 16 - layers), (0, 0), (0, 128 - part)))
    flat.append(norm.reshape(8, 2, 16, 256))
    *sums, norm_sum, squares = reduce_all(flat)
    kinds = len(grads[0])
    stacked = [jnp.stack([sums[l * kinds + i] for l in range(layers)]) for i in range(kinds)]
    halves = [(a[..., : a.shape[2] // 2], a[..., a.shape[2] // 2 :]) for a in stacked]
    keep = [jnp.where(first, a, b) for a, b in halves]
    give = [jnp.where(first, b, a) for a, b in halves]
    wide = other_core(jnp.concatenate(give[:3], axis=2))
    got = jnp.split(wide, (keep[0].shape[2], keep[0].shape[2] + keep[1].shape[2]), axis=2)
    got.append(other_core(give[3]))
    whole = [
        jnp.where(first, jnp.concatenate([a, b], axis=1), jnp.concatenate([b, a], axis=1))
        for a, b in zip(keep, got)
    ]
    return whole, norm_sum[:layers, :part].reshape(layers, 1, part), jnp.sum(squares)


def exchange_plan(seg_last, seg_before, seg_plane, reverse):
    dp = lax.axis_index("dp")
    z = dp // 2
    last = lax.dynamic_slice(seg_last, (z * 8,), (8,))
    before = lax.dynamic_slice(seg_before, (z * 8,), (8,))
    order = jnp.arange(8)
    inside = (before[:, None] == last[None, :]) & (order[:, None] > order[None, :])
    ends = seg_last[7::8]
    planes = jnp.arange(4)
    to_end = last == ends[z]
    back = (before[:, None] == ends[None, :]) & (planes[None, :] < z)
    coef = jnp.zeros((16, 16), jnp.float32)
    shift = jnp.arange(1, 4)
    if reverse:
        coef = coef.at[:8, :8].set(inside.T.astype(jnp.float32))
        source = (z - shift) % 4
        coef = coef.at[:8, 8:11].set((to_end[:, None] & (source > z)[None, :]).astype(jnp.float32))
        target = (z + shift) % 4
        coef = coef.at[9:12, :8].set(back[:, target].T.astype(jnp.float32))
    else:
        coef = coef.at[:8, :8].set(inside.astype(jnp.float32))
        source = (z - shift) % 4
        coef = coef.at[:8, 8:11].set(back[:, source].astype(jnp.float32))
        coef = coef.at[9:12, :8].set(jnp.broadcast_to(to_end.astype(jnp.float32), (3, 8)))
    return coef


class LocalPlan:
    def __init__(self, lengths, rows):
        me = lax.axis_index("dp") * 4 + lax.axis_index("head")
        first_row = me * rows
        seg, cos, sin, valid = stream_meta(lengths, first_row + jnp.arange(rows, dtype=jnp.int32))
        starts = jnp.arange(32, dtype=jnp.int32) * rows
        before = stream_meta(lengths, starts - 1)[0]
        last = stream_meta(lengths, starts + rows - 1)[0]
        follow = (seg == before[me]).astype(jnp.float32)
        tail = (seg == last[me]).astype(jnp.float32)
        place_ids = jnp.arange(rows)
        allowed = (seg[:, None] == seg[None, :]) & (place_ids[None, :] <= place_ids[:, None])
        close = cos[:, None] * cos[None, :] + sin[:, None] * sin[None, :]
        self.valid = valid
        self.weights = jnp.where(allowed, close, 0.0)
        zero = jnp.zeros_like(cos)
        self.aux = jnp.stack([cos, sin, follow, tail, valid, zero, zero, zero], axis=1)
        self.ahead = exchange_plan(last, before, None, False)
        self.behind = exchange_plan(last, before, None, True)

    def attend(self, q, k, v):
        ob, den, state = attend(q, k, v, self.weights, self.aux, self.ahead)
        return ob, (q, k, v, ob, den, state)

    def attend_back(self, kept, dob):
        q, k, v, ob, den, state = kept
        return attend_back(q, k, v, dob, ob, den, state, self.weights, self.aux, self.behind)


def block_attention(queries, key_rows, value_rows, weights, aux):
    cos, sin, tail = aux[:, 0], aux[:, 1], aux[:, 3]
    raw = jnp.einsum("ihe,jhe->hij", queries, key_rows, preferred_element_type=jnp.float32)
    scores = (raw * weights[None]).astype(jnp.bfloat16)
    num = jnp.einsum("hij,jhe->ihe", scores, value_rows, preferred_element_type=jnp.float32)
    den = jnp.transpose(jnp.sum(scores.astype(jnp.float32), axis=2))
    out = []
    for angle in (cos, sin):
        turned = key_rows.astype(jnp.float32) * (angle * tail)[:, None, None]
        out.append(
            jnp.einsum(
                "jhe,jhf->hef", turned, value_rows.astype(jnp.float32), precision=exact_mode
            )
        )
        out.append(jnp.sum(turned, axis=0))
    return num, den, tuple(out)


def finish_rows(queries, num, den, state, aux):
    cos, sin, follow = aux[:, 0], aux[:, 1], aux[:, 2]
    for angle, kv, ks in ((cos, state[0], state[1]), (sin, state[2], state[3])):
        turned = queries.astype(jnp.float32) * (angle * follow)[:, None, None]
        num = num + jnp.einsum("ihe,hef->ihf", turned, kv, precision=exact_mode)
        den = den + jnp.einsum("ihe,he->ih", turned, ks, precision=exact_mode)
    return num / jnp.maximum(den, 1.0)[:, :, None]


class WidePlan(LocalPlan):
    def __init__(self, lengths, rows):
        parts = lax.axis_size("dp") * lax.axis_size("head")
        me = lax.axis_index("dp") * lax.axis_size("head") + lax.axis_index("head")
        seg, cos, sin, valid = stream_meta(
            lengths, me * rows + jnp.arange(rows, dtype=jnp.int32)
        )
        starts = jnp.arange(parts, dtype=jnp.int32) * rows
        before = stream_meta(lengths, starts - 1)[0]
        last = stream_meta(lengths, starts + rows - 1)[0]
        follow = (seg == before[me]).astype(jnp.float32)
        tail = (seg == last[me]).astype(jnp.float32)
        place_ids = jnp.arange(rows)
        allowed = (seg[:, None] == seg[None, :]) & (place_ids[None, :] <= place_ids[:, None])
        close = cos[:, None] * cos[None, :] + sin[:, None] * sin[None, :]
        self.valid = valid
        self.weights = jnp.where(allowed, close, 0.0)
        self.aux = jnp.stack([cos, sin, follow, tail, valid], axis=1)
        devices = jnp.arange(parts)
        self.ahead = ((last == before[me]) & (devices < me)).astype(jnp.float32)
        self.behind = ((before == last[me]) & (devices > me)).astype(jnp.float32)

    def masked(self, state, coef):
        def one(a):
            everything = lax.all_gather(a.astype(jnp.bfloat16), ("dp", "head"))
            return jnp.einsum(
                "d,d...->...",
                coef.astype(jnp.bfloat16),
                everything,
                preferred_element_type=jnp.float32,
            )

        return jax.tree.map(one, state)

    def attend(self, q, k, v):
        rows, model = q.shape
        split = lambda a: a.reshape(rows, HEADS, model // HEADS)
        local = lambda *a: block_attention(*a, self.weights, self.aux)
        (num, den, state), pull = jax.vjp(local, split(q), split(k), split(v))
        state = self.masked(state, self.ahead)
        finish = lambda *a: finish_rows(*a, self.aux)
        out, finish_pull = jax.vjp(finish, split(q), num, den, state)
        return out.astype(jnp.bfloat16).reshape(rows, model), (pull, finish_pull)

    def attend_back(self, kept, dob):
        pull, finish_pull = kept
        rows, model = dob.shape
        grad = dob.astype(jnp.float32).reshape(rows, HEADS, model // HEADS)
        dq_one, dnum, dden, dstate = finish_pull(grad)
        dstate = self.masked(dstate, self.behind)
        dq, dk, dv = pull((dnum, dden, dstate))
        dq = dq.astype(jnp.float32) + dq_one.astype(jnp.float32)
        dk = dk.astype(jnp.float32) * self.valid[:, None, None]
        out = [a.reshape(rows, model).astype(jnp.bfloat16) for a in (dq, dk, dv)]
        return jnp.concatenate(out, axis=1)


def wide_gather(w_qkv, w_out, w_up, w_down, norm_params):
    fulls = []
    for a in (w_qkv, w_out, w_up, w_down):
        part = lax.all_gather(a.astype(jnp.bfloat16), "dp", axis=1, tiled=True)
        fulls.append(lax.all_gather(part, "head", axis=2, tiled=True))
    norm = lax.all_gather(norm_params.astype(jnp.bfloat16), "dp", axis=2, tiled=True)
    return fulls, lax.all_gather(norm, "head", axis=1, tiled=True)


def wide_reduce(grads, norm_grad):
    def one(a):
        part = lax.psum_scatter(a, "head", scatter_dimension=1, tiled=True)
        part = lax.psum_scatter(part.astype(jnp.float32), "dp", scatter_dimension=0, tiled=True)
        return part

    whole = [jnp.stack([one(layer[i]) for layer in grads]) for i in range(len(grads[0]))]
    part = lax.psum_scatter(norm_grad, "head", scatter_dimension=1, tiled=True)
    norm = lax.psum_scatter(part, "dp", scatter_dimension=2, tiled=True)
    squares = sum([jnp.sum(a * a) for a in whole + [norm]])
    return whole, norm, lax.psum(squares, ("dp", "head"))


def body(
    inputs, cotangent, lengths,
    w_qkv, m_qkv, v_qkv, w_out, m_out, v_out, w_up, m_up, v_up, w_down, m_down, v_down,
    norm_params, m_norm, v_norm,
):
    rows, model = inputs.shape
    layers = w_qkv.shape[0]
    near = lax.axis_size("dp") == 8 and lax.axis_size("head") == 4 and rows == 512
    plan = (LocalPlan if near else WidePlan)(lengths, rows)
    fulls, norm_full = (gather_plan if near else wide_gather)(
        w_qkv, w_out, w_up, w_down, norm_params
    )
    norm_full = norm_full.astype(jnp.float32)
    hidden = inputs.astype(jnp.float32)
    kept = []
    for layer in range(layers):
        qkv_w, out_w, up_w, down_w = (a[layer] for a in fulls)
        gains = norm_full[layer]
        acts = hidden.astype(jnp.bfloat16)
        mixed = jnp.dot(acts, qkv_w, preferred_element_type=jnp.float32)
        soft = jax.nn.softplus(mixed[:, : 2 * model]).astype(jnp.bfloat16)
        q = soft[:, :model]
        k = soft[:, model:] * plan.valid[:, None].astype(jnp.bfloat16)
        v = mixed[:, 2 * model :].astype(jnp.bfloat16)
        attended, attend_kept = plan.attend(q, k, v)
        first_in = hidden + jnp.dot(attended, out_w, preferred_element_type=jnp.float32)
        first_out = layer_norm(first_in, gains[0], gains[1])
        first_low = first_out.astype(jnp.bfloat16)
        inner = jnp.dot(first_low, up_w, preferred_element_type=jnp.float32)
        act = gelu_exact(inner).astype(jnp.bfloat16)
        second_in = first_out + jnp.dot(act, down_w, preferred_element_type=jnp.float32)
        kept.append((acts, mixed, attend_kept, attended, first_in, first_low, inner, act, second_in))
        hidden = layer_norm(second_in, gains[2], gains[3])
    grad_hidden = cotangent.astype(jnp.float32)
    grads = [None] * layers
    norm_grads = [None] * layers
    for layer in reversed(range(layers)):
        acts, mixed, attend_kept, attended, first_in, first_low, inner, act, second_in = kept[layer]
        qkv_w, out_w, up_w, down_w = (a[layer] for a in fulls)
        gains = norm_full[layer]
        _, pull_two = jax.vjp(layer_norm, second_in, gains[2], gains[3])
        grad_second, dgain_two, dshift_two = pull_two(grad_hidden)
        branch_two = grad_second.astype(jnp.bfloat16)
        dw_down = contract_rows(act, branch_two).astype(jnp.bfloat16)
        grad_act = contract_cols(branch_two, down_w)
        _, gelu_pull = jax.vjp(gelu_exact, inner)
        grad_inner = gelu_pull(grad_act)[0].astype(jnp.bfloat16)
        dw_up = contract_rows(first_low, grad_inner).astype(jnp.bfloat16)
        grad_first = grad_second + contract_cols(grad_inner, up_w)
        _, pull_one = jax.vjp(layer_norm, first_in, gains[0], gains[1])
        grad_first_in, dgain_one, dshift_one = pull_one(grad_first)
        branch = grad_first_in.astype(jnp.bfloat16)
        dw_out = contract_rows(attended, branch).astype(jnp.bfloat16)
        dob = contract_cols(branch, out_w).astype(jnp.bfloat16)
        grad_mixed = plan.attend_back(attend_kept, dob)
        slope = jax.nn.sigmoid(mixed[:, : 2 * model])
        grad_soft = (grad_mixed[:, : 2 * model].astype(jnp.float32) * slope).astype(jnp.bfloat16)
        grad_pre = jnp.concatenate([grad_soft, grad_mixed[:, 2 * model :]], axis=1)
        dw_qkv = contract_rows(acts, grad_pre).astype(jnp.bfloat16)
        grad_hidden = grad_first_in + contract_cols(grad_pre, qkv_w)
        grads[layer] = (dw_qkv, dw_out, dw_up, dw_down)
        norm_grads[layer] = jnp.stack([dgain_one, dshift_one, dgain_two, dshift_two])
    whole, norm_sum, squares = (reduce_plan if near else wide_reduce)(grads, jnp.stack(norm_grads))
    grad_norm = jnp.sqrt(squares)
    factor = clip_limit / jnp.maximum(grad_norm, clip_limit)
    new_qkv = adam_step(w_qkv, m_qkv, v_qkv, whole[0], factor, rate_matrix, decay_rate)
    new_out = adam_step(w_out, m_out, v_out, whole[1], factor, rate_outproj, decay_rate)
    new_up = adam_step(w_up, m_up, v_up, whole[2], factor, rate_matrix, decay_rate)
    new_down = adam_step(w_down, m_down, v_down, whole[3], factor, rate_matrix, decay_rate)
    new_norm = adam_step(norm_params, m_norm, v_norm, norm_sum, factor, rate_norm, 0.0)
    return (
        (hidden, grad_hidden, grad_norm.reshape(1))
        + new_qkv + new_out + new_up + new_down + new_norm
    )


def solution(mesh):
    rows = P(("dp", "head"), None)
    weight = P(None, "dp", "head")
    norm = P(None, "head", "dp")
    in_specs = (rows, rows, P()) + (weight,) * 12 + (norm,) * 3
    out_specs = (rows, rows, P()) + (weight,) * 12 + (norm,) * 3
    return jax.shard_map(body, mesh=mesh, in_specs=in_specs, out_specs=out_specs, check_vma=False)
```

time: 3180 us -> 604 us (0.19)
  waiting for transfers between devices: 1090 us -> 0.01 us
  blocking collectives: 746 us -> 0 us
  local copies, waits for them, and re-layouts: 571 us -> 36.4 us
  Pallas kernels: 0 us -> 374 us
  matrix products: 454 us -> 136 us
  other arithmetic: 191 us -> 48.5 us
  loops' own time: 47.2 us -> 0 us
    reduce_scatter x10 -> x0, waiting for transfers between devices: 747 us -> none  [the longest x2 325 us: body(): lax.psum_scatter(grad_set[2], 'dp', scatter_dimension=0, tiled=True)]
    all_gather x28 -> x0, blocking collectives: 627 us -> none  [the longest x8 203 us: carried_in(): lax.all_gather(a.astype(kind), axis)]
    pallas_call x0 -> x6, Pallas kernels: none -> 374 us  [the longest x1 150 us: reduce_all(): pl.pallas_call(functools.partial(reduce_kernel, dims), out_shape=[jax.Sha...]
    dot_general x223 -> x8, matrix products: 373 us -> 61.3 us  [the longest x2 40.8 us: body(): inner = jnp.dot(first_low, up_w, preferred_element_type=jnp.float32)]
    unnamed x34 -> x0, waiting for transfers between devices: 273 us -> none
    dynamic_update_slice x56 -> x0, local copies, waits for them, and re-layouts: 213 us -> none  [run_blocks(): lax.scan(jax.checkpoint(block_step), initial, (by_blocks(queries), by_blo...]
    convert_element_type x18 -> x1, local copies, waits for them, and re-layouts: 72.8 us -> 0.09 us  [body(): norm_full = norm_full.astype(jnp.float32)]
    unnamed x391 -> x137, local copies, waits for them, and re-layouts: 86 us -> 17.5 us
  transfers between devices with their start and end apart: 33 -> 4, of which waited for: 17 -> 0; matrix products, arithmetic and copies ran while one was open for 29% -> 9% of each run, Pallas kernels for 0% -> 0%
where the time goes in v1:
time: 604 us; the launch traced here: 600 us
  Pallas kernels  374 us (62%)
  matrix products  136 us (23%)
  other arithmetic  48.5 us (8%)
  local copies, waits for them, and re-layouts  36.4 us (6%)
    pallas_call x1, Pallas kernels, reduce_all(): pl.pallas_call(functools.partial(reduce_kernel, dims), out_shape=[jax.Sha...  150 us
    pallas_call x1, Pallas kernels, gather_all(): pl.pallas_call(functools.partial(gather_kernel, dims), out_shape=shapes,...  127 us
    pallas_call x2, Pallas kernels, attend(): pl.pallas_call(functools.partial(attend_kernel, pairs), out_shape=[jax.Sh...  50.2 us
    pallas_call x2, Pallas kernels, attend_back(): pl.pallas_call(functools.partial(attend_back_kernel, pairs), out_shape=ja...  45.8 us
    dot_general x8, matrix products, contract_cols(): lax.dot_general(left, right, (((1,), (1,)), ((), ())), preferred_element_...  43 us
    dot_general x2, matrix products, body(): inner = jnp.dot(first_low, up_w, preferred_element_type=jnp.float32)  40.8 us
    dot_general x8, matrix products, contract_rows(): lax.dot_general(left, right, (((0,), (0,)), ((), ())), preferred_element_...  32.1 us
    unnamed x137, local copies, waits for them, and re-layouts  17.5 us
  transfers between devices with their start and end apart: 4, of which 0 were waited for; matrix products, arithmetic and copies ran while one was open for 9% of the time, Pallas kernels for 0%

profile of v1, /device:TPU:0, one launch (start us, length us, event | category | flops | bytes accessed | tf_op | source)
XLA Modules:
  0.0 600.2 jit_solution(309509270877888656)
XLA Ops:
  35.4 127.2 %gather_weights.1 = (bf16[2,768,2304]{2,1,0:T(8,128)(2,1)}, bf16[2,768,768]{2,1,0:T(8,128)(2,1)}, bf16[2,768,3072]{2,1,0:T(8,128)(2,1)}, bf16[2,3072,768]{2,1,0:T(8,128)(2,1)}, bf16[1,256,256]{2,1,0:T(8,128)(2,1)}) custom-call(bf16[2,48,1152]{2,1,0:T(8,128)(2,1)} %maximum_select_fusion.5.refs_0_, bf16[2,48,384]{2,1,0:T(8,128)(2,1)} %maximum_select_fusion.7.refs_1_, ...), custom_call_target="tpu_custom_call" | custom-call | tf_op jit(solution)/shard_map/gather_weights/pallas_call | solution.py:160
  162.6 4.2 convolution_bitcast_fusion
  169.3 30.3 %attend.2 = (bf16[512,768]{1,0:T(8,128)(2,1)S(1)}, f32[512,128]{1,0:T(8,128)S(1)}, bf16[8,16,896]{2,1,0:T(8,128)(2,1)S(1)}) custom-call(f32[16,16]{1,0:T(8,128)S(1)} %scatter.37.coef, bf16[512,768]{1,0:T(8,128)(2,1)S(1)} %get-tuple-element.281.q_ref, bf16[512,768]{1,0:T(8,128)(2,1)S(1)} %get-tuple-element.280.k_ref, bf16[512,768]{1,0:T(8,128)(2,1)S(1)} %slice.578.v_ref, ...), custom_call_target="tpu_custom_call" | custom-call | tf_op jit(solution)/shard_map/attend/pallas_call | solution.py:595
  202.9 20.6 %multiply_convert_fusion.1 = (bf16[512,3072]{1,0:T(8,128)(2,1)S(1)}, f32[512,3072]{1,0:T(8,128)}, f32[512,3072]{1,0:T(8,128)}) fusion(bf16[2,768,3072]{2,1,0:T(8,128)(2,1)} %get-tuple-element.115, f32[512,768]{1,0:T(8,128)} %copy-done.12, f32[768]{0:T(1024)S(1)} %get-tuple-element.239, f32[768]{0:T(1024)S(1)} %get-tuple-element.240, f32[512]{0:T(512)S(1)} %fusion.105, ...), kind=kOutput, calls=%fused_computation.23 | convolution fusion | flops 2520121344 | bytes 22030336 | tf_op jit(solution)/shard_map/dot_general | solution.py:1040
  223.5 6.2 %fusion.147 = (f32[512]{0:T(512)S(1)}, f32[512,768]{1,0:T(8,128)S(1)}) fusion(bf16[512,3072]{1,0:T(8,128)(2,1)S(1)} %get-tuple-element.270, bf16[2,3072,768]{2,1,0:T(8,128)(2,1)} %get-tuple-element.116, f32[768]{0:T(1024)S(1)} %get-tuple-element.239, f32[768]{0:T(1024)S(1)} %get-tuple-element.240, f32[512]{0:T(512)S(1)} %fusion.105, ...), kind=kOutput, calls=%fused_computation.314 | convolution fusion | flops 2418277888 | bytes 11022336 | tf_op jit(solution)/shard_map/dot_general | solution.py:1042
  230.0 4.1 fusion.38
  236.1 19.9 %attend.3 = (bf16[512,768]{1,0:T(8,128)(2,1)S(1)}, f32[512,128]{1,0:T(8,128)S(1)}, bf16[8,16,896]{2,1,0:T(8,128)(2,1)S(1)}) custom-call(f32[16,16]{1,0:T(8,128)S(1)} %scatter.37.coef, bf16[512,768]{1,0:T(8,128)(2,1)S(1)} %get-tuple-element.279.q_ref, bf16[512,768]{1,0:T(8,128)(2,1)S(1)} %get-tuple-element.278.k_ref, bf16[512,768]{1,0:T(8,128)(2,1)S(1)} %slice.577.v_ref, ...), custom_call_target="tpu_custom_call" | custom-call | tf_op jit(solution)/shard_map/attend/pallas_call | solution.py:595
  258.7 20.2 %multiply_convert_fusion = (bf16[512,3072]{1,0:T(8,128)(2,1)S(1)}, f32[512,3072]{1,0:T(8,128)}, f32[512,3072]{1,0:T(8,128)}) fusion(bf16[2,768,3072]{2,1,0:T(8,128)(2,1)} %get-tuple-element.115, f32[512,768]{1,0:T(8,128)S(1)} %get-tuple-element.314, f32[768]{0:T(1024)S(1)} %get-tuple-element.235, f32[768]{0:T(1024)S(1)} %get-tuple-element.236, ...), kind=kOutput, calls=%fused_computation.10 | convolution fusion | flops 2520121344 | bytes 22030336 | tf_op jit(solution)/shard_map/dot_general | solution.py:1040
  278.9 2.7 fusion.149
  285.1 12.2 %add_convert_fusion.1 = bf16[512,3072]{1,0:T(8,128)(2,1)} fusion(f32[512,3072]{1,0:T(8,128)} %get-tuple-element.269, f32[512,3072]{1,0:T(8,128)} %get-tuple-element.315, bf16[2,3072,768]{2,1,0:T(8,128)(2,1)} %get-tuple-element.116, f32[512,768]{1,0:T(8,128)} %get-tuple-element.267, f32[512]{0:T(512)S(1)} %negate_multiply_fusion.5), kind=kOutput, calls=%fused_computation.9 | convolution fusion | flops 2438725632 | bytes 22022144 | tf_op jit(solution)/shard_map/dot_general | solution.py:776
  297.3 6.8 %multiply_reduce_fusion = (bf16[768]{0:T(1024)(128)(2,1)S(1)}, f32[512]{0:T(512)S(1)}, bf16[768]{0:T(1024)(128)(2,1)S(1)}, f32[512,768]{1,0:T(8,128)S(1)}) fusion(f32[512,768]{1,0:T(8,128)S(1)} %copy-done.15, f32[512]{0:T(512)S(1)} %fusion.107, f32[512]{0:T(512)S(1)} %broadcast_multiply_fusion.1, f32[768]{0:T(1024)S(1)} %get-tuple-element.236, ...), kind=kOutput, calls=%fused_computation.98 | convolution fusion | flops 2419849216 | bytes 12597248 | tf_op jit(solution)/shard_map/dot_general | solution.py:776
  306.7 23.2 %attend_back.2 = bf16[512,2304]{1,0:T(8,128)(2,1)} custom-call(f32[16,16]{1,0:T(8,128)S(1)} %scatter.41.coef, bf16[512,768]{1,0:T(8,128)(2,1)S(1)} %get-tuple-element.279.q_ref, bf16[512,768]{1,0:T(8,128)(2,1)S(1)} %get-tuple-element.278.k_ref, bf16[512,768]{1,0:T(8,128)(2,1)S(1)} %slice.577.v_ref, bf16[512,768]{1,0:T(8,128)(2,1)S(1)} %convolution_convert_fusion.9.dob_ref, ...), custom_call_target="tpu_custom_call" | custom-call | tf_op jit(solution)/shard_map/attend_back/pallas_call | solution.py:726
  333.6 4.7 convolution_convert_fusion
  338.3 4.8 convolution_convert_fusion.1
  347.5 4.1 convolution_convert_fusion.2
  353.5 4.4 convolution_convert_fusion.3
  357.9 8.2 %add_convert_fusion = bf16[512,3072]{1,0:T(8,128)(2,1)S(1)} fusion(f32[512,3072]{1,0:T(8,128)} %get-tuple-element.271, f32[512,3072]{1,0:T(8,128)} %get-tuple-element.310, bf16[2,3072,768]{2,1,0:T(8,128)(2,1)} %get-tuple-element.116, f32[512,768]{1,0:T(8,128)S(1)} %get-tuple-element.263, f32[512]{0:T(512)S(1)} %negate_multiply_fusion.3), kind=kOutput, calls=%fused_computation.8 | convolution fusion | flops 2438725632 | bytes 22022144 | tf_op jit(solution)/shard_map/dot_general | solution.py:776
  366.1 5.4 multiply_reduce_fusion.2
  371.5 5.3 convolution_convert_fusion.4
  381.4 22.6 %attend_back.3 = bf16[512,2304]{1,0:T(8,128)(2,1)} custom-call(f32[16,16]{1,0:T(8,128)S(1)} %scatter.41.coef, bf16[512,768]{1,0:T(8,128)(2,1)S(1)} %copy-done.5, bf16[512,768]{1,0:T(8,128)(2,1)S(1)} %copy-done.3, bf16[512,768]{1,0:T(8,128)(2,1)S(1)} %copy-done.1, bf16[512,768]{1,0:T(8,128)(2,1)S(1)} %convolution_convert_fusion.8.dob_ref, ...), custom_call_target="tpu_custom_call" | custom-call | tf_op jit(solution)/shard_map/attend_back/pallas_call | solution.py:726
  409.3 5.0 convolution_convert_fusion.5
  414.3 150.4 %reduce_gradients.1 = (f32[48,1152]{1,0:T(8,128)}, f32[48,384]{1,0:T(8,128)}, f32[48,1536]{1,0:T(8,128)}, f32[192,384]{1,0:T(8,128)}, f32[48,1152]{1,0:T(8,128)}...) custom-call(bf16[8,2,48,2304]{3,2,1,0:T(8,128)(2,1)} %bitcast.155, ...), custom_call_target="tpu_custom_call" | custom-call | tf_op jit(solution)/shard_map/reduce_gradients/pallas_call | solution.py:350
  574.3 6.4 %add_add_fusion.4 = f32[512,768]{1,0:T(8,128)} fusion(f32[512,768]{1,0:T(8,128)} %copy-done.23, bf16[2,768,2304]{2,1,0:T(8,128)(2,1)} %get-tuple-element.111, bf16[512,768]{1,0:T(8,128)(2,1)S(1)} %slice.354, bf16[512,1536]{1,0:T(8,128)(2,1)} %copy-done.24, f32[512]{0:T(512)S(1)} %negate_multiply_fusion.2), kind=kOutput, calls=%fused_computation.116 | convolution fusion | flops 1817444352 | bytes 9046016 | tf_op jit(solution)/shard_map/dot_general | solution.py:776
  583.3 3.0 multiply_subtract_fusion
  (294 shorter events, 94.2 us)
Async XLA Ops:
  2.1 9.7 %copy-start.10 = (f32[2,384,192]{2,1,0:T(8,128)}, f32[2,384,192]{2,1,0:T(8,128)S(1)}, u32[]{:S(2)}) copy-start(f32[2,384,192]{2,1,0:T(8,128)S(1)} %copy.130) | copy-start | bytes 1769476
  2.2 21.8 %copy-start.9 = (bf16[512,768]{1,0:T(8,128)(2,1)S(1)}, bf16[512,768]{1,0:T(8,128)(2,1)}, u32[]{:S(2)}) copy-start(bf16[512,768]{1,0:T(8,128)(2,1)} %param.31) | copy-start | bytes 2359300
  2.3 28.7 %collective-permute-start.1 = (bf16[2,192,192]{2,1,0:T(8,128)(2,1)S(1)}, bf16[2,192,192]{2,1,0:T(8,128)(2,1)}, u32[]{:S(2)}, u32[]{:S(2)}) collective-permute-start(bf16[2,192,192]{2,1,0:T(8,128)(2,1)S(1)} %get-tuple-element.289), channel_id=1, source_target_pairs={{0,1},{1,0},{2,3},{3,2},{4,5},{5,4},{6,7},{7,6},{8,9},{9,8},{10,11... | collective-permute-start | bytes 442376 | tf_op jit(solution)/shard_map/ppermute | solution.py:794
  3.1 29.8 %collective-permute-start = (bf16[2,48,1536]{2,1,0:T(8,128)(2,1)S(1)}, bf16[2,48,1536]{2,1,0:T(8,128)(2,1)S(1)}, u32[]{:S(2)}, u32[]{:S(2)}) collective-permute-start(bf16[2,48,1536]{2,1,0:T(8,128)(2,1)S(1)} %concatenate.74), channel_id=1, source_target_pairs={{0,1},{1,0},{2,3},{3,2},{4,5},{5,4},{6,7},{7,6},{8,9},{9,8},{10,11... | collective-permute-start | bytes 884744 | tf_op jit(solution)/shard_map/ppermute | solution.py:794
  169.1 30.6 %copy-start = (bf16[512,768]{1,0:T(8,128)(2,1)}, bf16[512,768]{1,0:T(8,128)(2,1)S(1)}, u32[]{:S(2)}) copy-start(bf16[512,768]{1,0:T(8,128)(2,1)S(1)} %slice.578.v_ref) | copy-start | bytes 2359300
  169.1 30.6 %copy-start.48 = (bf16[2,768,768]{2,1,0:T(8,128)(2,1)S(1)}, bf16[2,768,768]{2,1,0:T(8,128)(2,1)}, u32[]{:S(2)}) copy-start(bf16[2,768,768]{2,1,0:T(8,128)(2,1)} %get-tuple-element.113) | copy-start | bytes 7077892
  169.1 30.6 %copy-start.51 = (bf16[512,768]{1,0:T(8,128)(2,1)S(1)}, bf16[512,768]{1,0:T(8,128)(2,1)}, u32[]{:S(2)}) copy-start(bf16[512,768]{1,0:T(8,128)(2,1)} %param.30) | copy-start | bytes 2359300
  169.3 31.3 %copy-start.2 = (bf16[512,768]{1,0:T(8,128)(2,1)}, bf16[512,768]{1,0:T(8,128)(2,1)S(1)}, u32[]{:S(2)}) copy-start(bf16[512,768]{1,0:T(8,128)(2,1)S(1)} %get-tuple-element.280.k_ref) | copy-start | bytes 2359300
  169.3 31.3 %copy-start.4 = (bf16[512,768]{1,0:T(8,128)(2,1)}, bf16[512,768]{1,0:T(8,128)(2,1)S(1)}, u32[]{:S(2)}) copy-start(bf16[512,768]{1,0:T(8,128)(2,1)S(1)} %get-tuple-element.281.q_ref) | copy-start | bytes 2359300
  202.9 20.6 %copy-start.13 = (f32[512,768]{1,0:T(8,128)S(1)}, f32[512,768]{1,0:T(8,128)}, u32[]{:S(2)}) copy-start(f32[512,768]{1,0:T(8,128)} %copy-done.12) | copy-start | bytes 4718596
  256.0 22.9 %slice-start.2 = ((s8[9437184]{0:T(1024)(128)(4,1)}), s8[4194304]{0:T(1024)(128)(4,1)S(1)}, s32[]{:S(2)}) async-start(s8[9437184]{0:T(1024)(128)(4,1)} %bitcast.176), calls=%async_computation.2 | async-start | bytes 8388608
  258.3 20.6 %copy-start.14 = (f32[512,768]{1,0:T(8,128)}, f32[512,768]{1,0:T(8,128)S(1)}, u32[]{:S(2)}) copy-start(f32[512,768]{1,0:T(8,128)S(1)} %get-tuple-element.314) | copy-start | bytes 4718596
  258.6 20.3 %slice-start.3 = ((s8[9437184]{0:T(1024)(128)(4,1)}), s8[4194304]{0:T(1024)(128)(4,1)S(1)}, s32[]{:S(2)}) async-start(s8[9437184]{0:T(1024)(128)(4,1)} %bitcast.176), calls=%async_computation.3 | async-start | bytes 8388608
  258.7 20.3 %slice-start.4 = ((s8[9437184]{0:T(1024)(128)(4,1)}), s8[1048576]{0:T(1024)(128)(4,1)S(1)}, s32[]{:S(2)}) async-start(s8[9437184]{0:T(1024)(128)(4,1)} %bitcast.176), calls=%async_computation.4 | async-start | bytes 2097152
  285.1 12.2 %copy-start.15 = (f32[512,768]{1,0:T(8,128)S(1)}, f32[512,768]{1,0:T(8,128)}, u32[]{:S(2)}) copy-start(f32[512,768]{1,0:T(8,128)} %copy-done.14) | copy-start | bytes 4718596
  333.6 11.4 %slice-start.5 = ((s8[7077888]{0:T(1024)(128)(4,1)}), s8[4194304]{0:T(1024)(128)(4,1)S(1)}, s32[]{:S(2)}) async-start(s8[7077888]{0:T(1024)(128)(4,1)} %bitcast.178), calls=%async_computation.5 | async-start | bytes 8388608
  371.5 32.5 %slice-start = ((s8[4718592]{0:T(1024)(128)(4,1)}), s8[4194304]{0:T(1024)(128)(4,1)S(1)}, s32[]{:S(2)}) async-start(s8[4718592]{0:T(1024)(128)(4,1)} %bitcast.148), calls=%async_computation | async-start | bytes 8388608
  376.9 27.2 %slice-start.1 = ((s8[4718592]{0:T(1024)(128)(4,1)}), s8[524288]{0:T(1024)(128)(4,1)S(1)}, s32[]{:S(2)}) async-start(s8[4718592]{0:T(1024)(128)(4,1)} %bitcast.148), calls=%async_computation.1 | async-start | bytes 1048576
  567.1 16.2 %collective-permute-start.3 = (f32[2,192,192]{2,1,0:T(8,128)}, f32[2,192,192]{2,1,0:T(8,128)}, u32[]{:S(2)}, u32[]{:S(2)}) collective-permute-start(f32[2,192,192]{2,1,0:T(8,128)} %get-tuple-element.282), channel_id=1, source_target_pairs={{0,1},{1,0},{2,3},{3,2},{4,5},{5,4},{6,7},{7,6},{8,9},{9,8},{10,11... | collective-permute-start | bytes 884744 | tf_op jit(solution)/shard_map/ppermute | solution.py:794
  573.8 8.2 %copy-start.46 = (f32[2,1,96]{2,1,0:T(1,128)S(1)}, f32[2,1,96]{2,1,0:T(1,128)}, u32[]{:S(2)}) copy-start(f32[2,1,96]{2,1,0:T(1,128)} %param.46) | copy-start | bytes 2308
  573.8 9.5 %copy-start.11 = (f32[2,384,192]{2,1,0:T(8,128)S(1)}, f32[2,384,192]{2,1,0:T(8,128)}, u32[]{:S(2)}) copy-start(f32[2,384,192]{2,1,0:T(8,128)} %copy-done.10) | copy-start | bytes 1769476
  573.8 9.5 %copy-start.17 = (f32[2,384,192]{2,1,0:T(8,128)S(1)}, f32[2,384,192]{2,1,0:T(8,128)}, u32[]{:S(2)}) copy-start(f32[2,384,192]{2,1,0:T(8,128)} %copy.139) | copy-start | bytes 1769476
  573.8 9.5 %copy-start.18 = (f32[2,384,192]{2,1,0:T(8,128)S(1)}, f32[2,384,192]{2,1,0:T(8,128)}, u32[]{:S(2)}) copy-start(f32[2,384,192]{2,1,0:T(8,128)} %copy.141) | copy-start | bytes 1769476
  573.8 18.1 %collective-permute-start.2 = (f32[2,48,1536]{2,1,0:T(8,128)}, f32[2,48,1536]{2,1,0:T(8,128)}, u32[]{:S(2)}, u32[]{:S(2)}) collective-permute-start(f32[2,48,1536]{2,1,0:T(8,128)} %concatenate.85), channel_id=1, source_target_pairs={{0,1},{1,0},{2,3},{3,2},{4,5},{5,4},{6,7},{7,6},{8,9},{9,8},{10,11... | collective-permute-start | bytes 1769480 | tf_op jit(solution)/shard_map/ppermute | solution.py:794
  (45 other events, 173.4 us)

commit v2 on v1

v2 whole, which is shorter than its diff:
```python
import functools
import math
from typing import Any, NamedTuple

import jax
import jax.numpy as jnp
from jax import lax
from jax.experimental import pallas as pl
from jax.experimental.pallas import tpu as pltpu
from jax.sharding import PartitionSpec as P

HEADS = 12
LONGEST = 8192
HD = 64

exact_mode = lax.Precision.HIGHEST
beta_one = 0.9
beta_two = 0.999
adam_eps = 1e-08
decay_rate = 0.1
rate_matrix = 0.1
rate_outproj = 0.5
rate_norm = 0.5
clip_limit = 1.0
norm_eps = 1e-05
step_fixed = 10.0

MESH = pl.DeviceIdType.MESH
FIRST_X = (0, 3)
NORM, QKV, OUT, UP, DOWN = range(5)
MATRICES = (QKV, OUT, UP, DOWN)
BY_Z, BY_X, BY_Y, BY_CORE, BY_CORNER, ON_X, ON_Y, ON_CORNER = range(8)
CORE, ONE, TWO, LAST = range(4)


def place():
    dp, hd = lax.axis_index("dp"), lax.axis_index("head")
    return dp // 2, dp % 2, hd // 2, hd % 2


def at(z, x, y, c):
    return (z * 2 + x, y * 2 + c)


def flip(x, y, c, d):
    dx, dy, dc = d // 4, (d // 2) % 2, d % 2
    return 1 - x if dx else x, 1 - y if dy else y, 1 - c if dc else c


def partners():
    z, x, y, c = place()
    out = [at((z + d) % 4, x, y, c) for d in (1, 2, 3)]
    return out + [at(z, *flip(x, y, c, d)) for d in range(1, 8)]


def greet():
    barrier = pltpu.get_barrier_semaphore()
    devices = partners()
    for dev in devices:
        pl.semaphore_signal(barrier, inc=1, device_id=dev, device_id_type=MESH)
    pl.semaphore_wait(barrier, len(devices))


class Links:
    def __init__(self, send_sem, recv_sem):
        self.send_sem, self.recv_sem, self.copies = send_sem, recv_sem, []
        self.left = set()

    def send(self, src, dst, dev):
        k = len(self.copies)
        copy = pltpu.make_async_remote_copy(
            src_ref=src,
            dst_ref=dst,
            send_sem=self.send_sem.at[k],
            recv_sem=self.recv_sem.at[k],
            device_id=dev,
            device_id_type=MESH,
        )
        copy.start()
        self.copies.append(copy)
        self.left.add(k)
        copy.number = k
        return copy

    def sent(self, copy):
        copy.wait_send()
        self.left.discard(copy.number)

    def finish(self):
        for k in sorted(self.left):
            self.copies[k].wait_send()


class Moves:
    def __init__(self, sem):
        self.sem, self.copies = sem, []
        self.left = []

    def start(self, src, dst):
        copy = pltpu.make_async_copy(src, dst, self.sem.at[len(self.copies)])
        copy.start()
        self.copies.append(copy)
        self.left.append(copy)
        return copy

    def wait(self, copy):
        if any(copy is other for other in self.left):
            copy.wait()
        self.left = [other for other in self.left if other is not copy]

    def finish(self):
        for copy in self.left:
            copy.wait()
        self.left = []


def region(kind, rows, cols, z, x, y, c):
    strip, head = z * 2 + x, y * 2 + c
    if kind in (QKV, OUT, NORM):
        first, left = (strip * 2 + c) * rows, y * cols
    elif kind == UP:
        first, left = strip * rows, head * cols
    else:
        first, left = head * rows, strip * cols
    return (
        pl.ds(pl.multiple_of(first, rows), rows),
        pl.ds(pl.multiple_of(left, cols), cols),
    )


def whole_shape(kind, rows, cols):
    if kind in (QKV, OUT, NORM):
        return rows * 16, cols * 2
    if kind == UP:
        return rows * 8, cols * 4
    return rows * 4, cols * 8


class Kept(NamedTuple):
    acts: Any
    slope: Any
    soft: Any
    ob: Any
    den: Any
    state: Any
    xh1: Any
    xh2: Any
    rstd: Any
    n1b: Any
    gz: Any
    gu: Any


class Gather:
    def __init__(self, kind, piece, full, links, moves):
        self.kind, self.piece, self.full = kind, piece, full
        self.links, self.moves = links, moves
        self.z, self.x, self.y, self.c = place()
        self.copies = {}

    def spot(self, zz, xx, yy):
        rows, cols = self.piece.shape
        span = region(self.kind, rows, cols, zz, xx, yy, self.c)
        return self.full.at[span[0], span[1]]

    def origin(self, d):
        return (self.z + 4 - d) % 4 if d else self.z

    def begin(self, d):
        z, x, y, c = self.z, self.x, self.y, self.c
        if d:
            dev = at((z + d) % 4, x, y, c)
            self.copies[BY_Z, d] = self.links.send(self.piece, self.spot(z, x, y), dev)
        else:
            self.own = self.moves.start(self.piece, self.spot(z, x, y))

    def fan(self, d):
        z, x, y, c = self.z, self.x, self.y, self.c
        if d:
            self.copies[BY_Z, d].wait_recv()
        here = self.spot(self.origin(d), x, y)
        src = here if d else self.piece
        self.copies[BY_X, d] = self.links.send(src, here, at(z, 1 - x, y, c))
        self.copies[BY_Y, d] = self.links.send(src, here, at(z, x, 1 - y, c))
        self.copies[BY_CORE, d] = self.links.send(src, here, at(z, x, y, 1 - c))

    def second(self, d):
        z, x, y, c = self.z, self.x, self.y, self.c
        from_x, from_y = self.spot(self.origin(d), 1 - x, y), self.spot(self.origin(d), x, 1 - y)
        self.copies[BY_X, d].wait_recv()
        if d in FIRST_X:
            self.copies[BY_CORNER, d] = self.links.send(from_x, from_x, at(z, x, 1 - y, c))
        self.copies[ON_X, d] = self.links.send(from_x, from_x, at(z, x, y, 1 - c))
        self.copies[BY_Y, d].wait_recv()
        if d not in FIRST_X:
            self.copies[BY_CORNER, d] = self.links.send(from_y, from_y, at(z, 1 - x, y, c))
        self.copies[ON_Y, d] = self.links.send(from_y, from_y, at(z, x, y, 1 - c))

    def third(self, d):
        z, x, y, c = self.z, self.x, self.y, self.c
        block = self.spot(self.origin(d), 1 - x, 1 - y)
        self.copies[BY_CORNER, d].wait_recv()
        self.copies[ON_CORNER, d] = self.links.send(block, block, at(z, x, y, 1 - c))

    def ready(self):
        for key in (BY_CORE, ON_X, ON_Y, ON_CORNER):
            for d in range(4):
                self.copies[key, d].wait_recv()
        self.moves.wait(self.own)


class Exchange:
    def __init__(self, coef, refs, links, reverse):
        self.coef, self.reverse, self.links = coef, reverse, links
        self.mine, self.got, self.sums, self.got_z, self.back, self.result = refs
        self.z, self.x, self.y, self.c = place()
        self.index = self.x * 4 + self.y * 2 + self.c

    def scatter(self):
        self.got[self.index] = self.mine[self.index]
        self.first = []
        for d in range(1, 8):
            nx, ny, nc = flip(self.x, self.y, self.c, d)
            src = self.mine.at[nx * 4 + ny * 2 + nc]
            dev = at(self.z, nx, ny, nc)
            self.first.append(self.links.send(src, self.got.at[self.index], dev))

    def across(self):
        for copy in self.first:
            copy.wait_recv()
        self.planes = []
        for d in (1, 2, 3):
            total = jnp.zeros(self.got.shape[1:], jnp.float32)
            for j in range(8):
                total = total + self.coef[8 + d, j] * self.got[j].astype(jnp.float32)
            self.sums[d - 1] = total.astype(jnp.bfloat16)
            dev = at((self.z + d) % 4, self.x, self.y, self.c)
            self.planes.append(self.links.send(self.sums.at[d - 1], self.got_z.at[d - 1], dev))

    def gather(self):
        for copy in self.planes:
            copy.wait_recv()
        parts = [self.got[j].astype(jnp.float32) for j in range(8)]
        parts += [self.got_z[d].astype(jnp.float32) for d in range(3)]
        for i in range(8):
            total = jnp.zeros(self.got.shape[1:], jnp.float32)
            span = range(i + 1, 8) if self.reverse else range(i)
            for j in list(span) + [8, 9, 10]:
                total = total + self.coef[i, j] * parts[j]
            self.back[i] = total.astype(jnp.bfloat16)
        self.result[self.index] = self.back[self.index]
        self.last = []
        for d in range(1, 8):
            nx, ny, nc = flip(self.x, self.y, self.c, d)
            src = self.back.at[nx * 4 + ny * 2 + nc]
            dev = at(self.z, nx, ny, nc)
            self.last.append(self.links.send(src, self.result.at[self.index], dev))

    def finish(self):
        for copy in self.last:
            copy.wait_recv()


def exchange_scratch(width):
    counts = (8, 8, 3, 3, 8, 8)
    return [pltpu.VMEM((n, 16, width), jnp.bfloat16) for n in counts]


def mm(a, b):
    return lax.dot_general(a, b, (((1,), (0,)), ((), ())), preferred_element_type=jnp.float32)


def mm_nt(a, b):
    return lax.dot_general(a, b, (((1,), (1,)), ((), ())), preferred_element_type=jnp.float32)


def mm_tn(a, b):
    return lax.dot_general(a, b, (((0,), (0,)), ((), ())), preferred_element_type=jnp.float32)


def low_lanes(shape):
    return lax.broadcasted_iota(jnp.int32, shape, len(shape) - 1) < HD


def lane_is(shape, h):
    return lax.broadcasted_iota(jnp.int32, shape, len(shape) - 1) == h


def pair_cols(p):
    return slice(p * 128, (p + 1) * 128)


def pack_state(ref, p, kind, block, extra):
    low = low_lanes((64, 128))
    packed = jnp.where(low, block[:64, :128], block[64:, :128]).astype(jnp.bfloat16)
    for s in range(4):
        ref[kind * 4 + s, :, pair_cols(p)] = packed[s * 16 : (s + 1) * 16]
    if extra is None:
        extra = jnp.zeros((64, 128), jnp.float32)
    extra = extra + jnp.where(lane_is((64, 128), 2 * p), block[:64, 128:], 0.0)
    return extra + jnp.where(lane_is((64, 128), 2 * p + 1), block[64:, 128:], 0.0)


def store_extra(ref, kind, extra, width):
    extra = extra.astype(jnp.bfloat16)
    for s in range(4):
        ref[kind * 4 + s, :, width - 128 :] = extra[s * 16 : (s + 1) * 16]


def unpack_state(ref, p, kind, width):
    packed = jnp.concatenate([ref[kind * 4 + s, :, pair_cols(p)] for s in range(4)], axis=0)
    sums = jnp.concatenate([ref[kind * 4 + s, :, width - 128 :] for s in range(4)], axis=0)
    low = low_lanes((64, 128))
    zero = jnp.zeros((64, 128), jnp.bfloat16)
    top = jnp.concatenate(
        [jnp.where(low, packed, zero), jnp.where(lane_is((64, 128), 2 * p), sums, zero)], axis=1
    )
    bottom = jnp.concatenate(
        [jnp.where(low, zero, packed), jnp.where(lane_is((64, 128), 2 * p + 1), sums, zero)],
        axis=1,
    )
    return jnp.concatenate([top, bottom], axis=0)


def spread(values, p):
    rows = values.shape[0]
    first = jnp.broadcast_to(values[:, 2 * p : 2 * p + 1], (rows, 128))
    second = jnp.broadcast_to(values[:, 2 * p + 1 : 2 * p + 2], (rows, 128))
    return jnp.where(low_lanes((rows, 128)), first, second)


def assemble_gains(full, layers):
    spots = lax.broadcasted_iota(jnp.int32, (128, 768), 0)
    lanes = lax.broadcasted_iota(jnp.int32, (128, 768), 1)
    total = jnp.zeros((64, 768), jnp.float32)
    for dp in range(8):
        both = full[dp * 32 : (dp + 1) * 32, :]
        left = jnp.concatenate([both[:, :128], both[:, 128:]], axis=0)
        put = jnp.where((lanes == spots + dp * 96) & (spots < 96), 1.0, 0.0).astype(jnp.bfloat16)
        total = total + mm(left, put)
    return [
        jnp.concatenate([total[head * 16 + i : head * 16 + i + 1] for head in range(4)], axis=0)
        for i in range(layers)
    ]


AHEAD, SECOND, THIRD = 6, 4, 8
PUMP = 4


def forward_kernel(layers, pairs, coef, x_ref, w_ref, aux_ref, *refs):
    order = (NORM,) + MATRICES
    pieces = refs[:5]
    h_out, gains_out = refs[5:7]
    refs = refs[7:]
    full_out = [(None,) + refs[4 * i : 4 * i + 4] for i in range(layers)]
    refs = refs[4 * layers :]
    saved = [Kept(*refs[12 * i : 12 * i + 12]) for i in range(layers)]
    rest = refs[12 * layers :]
    full = [(rest[0],) + rest[1 + 4 * i : 5 + 4 * i] for i in range(layers)]
    rest = rest[1 + 4 * layers :]
    hold = Kept(*rest[:5], None, *rest[5:11])
    num, n1, h_mid = rest[11:14]
    ex_refs = [rest[14 + 6 * i : 20 + 6 * i] for i in range(layers)]
    send_sem, recv_sem, move_sem = rest[-3:]
    rows, model = x_ref.shape
    half = rows // 2
    width = model + 128
    links, moves = Links(send_sem, recv_sem), Moves(move_sem)
    greet()
    norms = Gather(NORM, pieces[NORM], full[0][NORM], links, moves)
    every = [
        [norms]
        + [Gather(k, pieces[k].at[i], full[i][k], links, moves) for k in MATRICES]
        for i in range(layers)
    ]

    steps = []

    done = [0]

    def pump(n):
        while n > 0 and done[0] < len(steps):
            steps[done[0]]()
            done[0] += 1
            n -= 1

    def until(mark):
        pump(mark - done[0])

    chain = [part for parts in every for part in parts[1:]]
    chain.insert(2, norms)
    line = [(part, d) for part in chain for d in (0, 1, 3, 2)]
    marks = {}
    for i in range(-AHEAD, len(line) + THIRD):
        for stage, lag in ((0, -AHEAD), (1, 0), (2, SECOND), (3, THIRD)):
            if 0 <= i - lag < len(line):
                part, d = line[i - lag]
                steps.append(functools.partial((part.begin, part.fan, part.second, part.third)[stage], d))
                marks[id(part)] = len(steps)

    cos, sin = aux_ref[:, 0:1], aux_ref[:, 1:2]
    follow, tail, valid = aux_ref[:, 2:3], aux_ref[:, 3:4], aux_ref[:, 4:5]
    soft = hold.soft

    def q_of(p):
        return soft[:, p * 128 : (p + 1) * 128]

    def k_of(p):
        return soft[:, model + p * 128 : model + (p + 1) * 128]

    def v_of(p):
        return soft[:, 2 * model + p * 128 : 2 * model + (p + 1) * 128]

    def one_layer(layer):
        parts, whole, keep = every[layer], full[layer], saved[layer]
        mark = [marks[id(part)] for part in parts]
        h_ref = h_mid if layer else x_ref
        h_next = h_out if layer == layers - 1 else h_mid
        ex = Exchange(coef, ex_refs[layer], links, False)
        hold.acts[...] = h_ref[...].astype(jnp.bfloat16)
        moves.start(hold.acts, keep.acts)
        until(mark[QKV])
        parts[QKV].ready()
        moves.start(whole[QKV], full_out[layer][QKV])
        acts = hold.acts[...]
        for j in range(3 * model // 256):
            span = slice(j * 256, (j + 1) * 256)
            p = mm(acts, whole[QKV][:, span])
            if j * 256 < 2 * model:
                t = jnp.exp(-jnp.abs(p))
                hold.slope[:, span] = (jnp.where(p >= 0, 1.0, t) / (1.0 + t)).astype(jnp.bfloat16)
                p = jnp.maximum(p, 0.0) + jnp.log1p(t)
                if j * 256 >= model:
                    p = p * valid
            soft[:, span] = p.astype(jnp.bfloat16)
            if j % 3 == 2:
                pump(1)
        moves.start(hold.slope, keep.slope)
        moves.start(soft, keep.soft)

        ones = jnp.ones((rows, 128), jnp.bfloat16)
        extras = [None, None]
        for p in range(pairs):
            kp = k_of(p).astype(jnp.float32) * tail
            rhs = jnp.concatenate([v_of(p), ones], axis=1)
            for kind, angle in enumerate((cos, sin)):
                block = mm_tn((kp * angle).astype(jnp.bfloat16), rhs)
                extras[kind] = pack_state(ex.mine, p, kind, block, extras[kind])
        for kind in range(2):
            store_extra(ex.mine, kind, extras[kind], width)
        ex.scatter()
        den_ref = hold.den

        def inner(p):
            kp, vp = k_of(p), v_of(p)
            low = low_lanes((rows, 128))
            zero = jnp.zeros((rows, 128), jnp.bfloat16)
            out = []
            for e in range(2):
                qh = jnp.where(low if e == 0 else ~low, q_of(p), zero)
                mark_head = lane_is((rows, 128), 2 * p + e).astype(jnp.bfloat16)
                rhs = jnp.concatenate([vp, mark_head], axis=1)
                top = mm_nt(qh[:half], kp[:half]) * w_ref[:half, :half]
                bottom = mm_nt(qh[half:], kp) * w_ref[half:, :]
                top, bottom = top.astype(jnp.bfloat16), bottom.astype(jnp.bfloat16)
                out.append(jnp.concatenate([mm(top, rhs[:half]), mm(bottom, rhs)], axis=0))
            num[:, pair_cols(p)] = jnp.where(low, out[0][:, :128], out[1][:, :128])
            dens = out[0][:, 128:] + out[1][:, 128:]
            if p == 0:
                den_ref[...] = dens
            else:
                den_ref[...] += dens

        for p in range(pairs):
            inner(p)
            if p == 1:
                ex.across()
            if p == 3:
                ex.gather()
            pump(PUMP)
        ex.finish()
        moves.start(ex.result, keep.state)
        den = den_ref[...]
        cf, sf = cos * follow, sin * follow
        for p in range(pairs):
            qp = q_of(p)
            extra = cf * mm(qp, unpack_state(ex.result, p, 0, width))
            extra += sf * mm(qp, unpack_state(ex.result, p, 1, width))
            num[:, pair_cols(p)] += extra[:, :128]
            den = den + extra[:, 128:]
        den_ref[...] = den
        moves.start(hold.den, keep.den)
        inv = 1.0 / jnp.maximum(den, 1.0)
        ob = hold.ob
        for p in range(pairs):
            ob[:, pair_cols(p)] = (num[:, pair_cols(p)] * spread(inv, p)).astype(jnp.bfloat16)
        moves.start(hold.ob, keep.ob)
        until(mark[OUT])
        parts[OUT].ready()
        moves.start(whole[OUT], full_out[layer][OUT])

        def norm(x_ref, which, low_ref, whole_ref):
            gain, shift = gains[2 * which], gains[2 * which + 1]
            for i in range(0, rows, 128):
                x = x_ref[i : i + 128, :]
                centered = x - jnp.mean(x, axis=1, keepdims=True)
                variance = jnp.mean(centered * centered, axis=1, keepdims=True)
                r = lax.rsqrt(variance + norm_eps)
                xh = centered * r
                x_ref[i : i + 128, :] = xh
                new = jnp.broadcast_to(r, (128, 128))
                if which:
                    new = jnp.where(low_lanes((128, 128)), hold.rstd[i : i + 128, :], new)
                hold.rstd[i : i + 128, :] = new
                y = xh * gain + shift
                whole_ref[i : i + 128, :] = y
                if low_ref is not None:
                    low_ref[i : i + 128, :] = y.astype(jnp.bfloat16)

        if layer == 0:
            until(mark[NORM])
            norms.ready()
            for i, lines in enumerate(assemble_gains(whole[NORM], layers)):
                gains_out[i, 0:4, :] = lines
                gains_out[i, 4:8, :] = jnp.zeros((4, model), jnp.float32)
        gains = [gains_out[layer, i : i + 1, :] for i in range(4)]
        attended = ob[...]
        for j in range(model // 256):
            span = slice(j * 256, (j + 1) * 256)
            first_in = h_ref[:, span].astype(jnp.float32)
            hold.xh1[:, span] = first_in + mm(attended, whole[OUT][:, span])
        norm(hold.xh1, 0, hold.n1b, n1)
        moves.start(hold.xh1, keep.xh1)
        moves.start(hold.n1b, keep.n1b)
        until(mark[UP])
        parts[UP].ready()
        moves.start(whole[UP], full_out[layer][UP])
        n1b = hold.n1b[...]
        hidden = whole[UP].shape[1]
        for j in range(hidden // 256):
            span = slice(j * 256, (j + 1) * 256)
            u = mm(n1b, whole[UP][:, span])
            phi = 0.5 * (1.0 + lax.erf(u * math.sqrt(0.5)))
            hold.gz[:, span] = (u * phi).astype(jnp.bfloat16)
            bell = jnp.exp(-0.5 * u * u) * (1.0 / math.sqrt(2.0 * math.pi))
            hold.gu[:, span] = (phi + u * bell).astype(jnp.bfloat16)
            pump(1)
        moves.start(hold.gz, keep.gz)
        moves.start(hold.gu, keep.gu)
        until(mark[DOWN])
        parts[DOWN].ready()
        moves.start(whole[DOWN], full_out[layer][DOWN])
        gz = hold.gz[...]
        for j in range(model // 256):
            span = slice(j * 256, (j + 1) * 256)
            hold.xh2[:, span] = n1[:, span] + mm_nt(gz, whole[DOWN][span, :])
        norm(hold.xh2, 1, None, h_next)
        moves.start(hold.xh2, keep.xh2)
        moves.start(hold.rstd, keep.rstd)
        moves.finish()

    for layer in range(layers):
        one_layer(layer)
    links.finish()


def forward(number, coef, inputs, weights, aux, pieces):
    rows, model = inputs.shape
    layers = pieces[1].shape[0]
    order = (NORM,) + MATRICES
    fulls = [whole_shape(k, *p.shape[-2:]) for k, p in zip(order, pieces)]
    hidden = fulls[UP][1]
    width = model + 128
    low, wide = jnp.bfloat16, jnp.float32
    kept = Kept(
        acts=((rows, model), low),
        slope=((rows, 2 * model), low),
        soft=((rows, 3 * model), low),
        ob=((rows, model), low),
        den=((rows, 128), wide),
        state=((8, 16, width), low),
        xh1=((rows, model), wide),
        xh2=((rows, model), wide),
        rstd=((rows, 128), wide),
        n1b=((rows, model), low),
        gz=((rows, hidden), low),
        gu=((rows, hidden), low),
    )
    vmem = pl.BlockSpec(memory_space=pltpu.VMEM)
    anywhere = pl.BlockSpec(memory_space=pl.ANY)
    scratch = [pltpu.VMEM(s, low) for s in fulls[:1] + fulls[1:] * layers]
    scratch += [pltpu.VMEM(*a) for a in kept[:5] + kept[6:]]
    scratch += [pltpu.VMEM((rows, model), wide)] * 3
    scratch += exchange_scratch(width) * layers
    scratch += [pltpu.SemaphoreType.DMA((layers * 141 + 31,))] * 2
    scratch += [pltpu.SemaphoreType.DMA((layers * 22,))]
    outs = pl.pallas_call(
        functools.partial(forward_kernel, layers, model // 128),
        out_shape=[
            jax.ShapeDtypeStruct((rows, model), wide),
            jax.ShapeDtypeStruct((layers, 8, model), wide),
        ]
        + [jax.ShapeDtypeStruct(s, low) for s in fulls[1:]] * layers
        + [jax.ShapeDtypeStruct(s, t) for s, t in kept] * layers,
        in_specs=[pl.BlockSpec(memory_space=pltpu.SMEM)] + [vmem] * 3 + [anywhere] * 5,
        out_specs=[vmem] * 2 + [anywhere] * (layers * (4 + len(kept))),
        scratch_shapes=scratch,
        compiler_params=pltpu.CompilerParams(
            collective_id=number, has_side_effects=True, vmem_limit_bytes=61 * 2**20
        ),
        name="forward_layers",
    )(coef, inputs, weights, aux, *pieces)
    outs, h_out, gains = outs[2:], outs[0], outs[1]
    held = []
    for i in range(layers):
        held.append((gains[i], outs[4 * i : 4 * i + 4], Kept(*outs[4 * layers + 12 * i :][:12])))
    return h_out, held


class Reduce:
    def __init__(self, own, core_in, one_y, one_x, two, from_z, links):
        self.own, self.core_in, self.links = own, core_in, links
        self.one_y, self.one_x, self.two, self.from_z = one_y, one_x, two, from_z
        self.z, self.x, self.y, self.c = place()
        self.rows, self.cols = two.shape[1], two.shape[2]
        self.copies = {}

    def plane(self, d):
        return (self.z + d) % 4 if d else self.z

    def side(self, yy):
        return pl.ds(pl.multiple_of(yy * self.cols, self.cols), self.cols)

    def strip(self, number, count=1):
        return pl.ds(pl.multiple_of(number * self.rows, self.rows), count * self.rows)

    def both(self, d):
        return self.strip(self.plane(d) * 2, 2)

    def give(self, ref, d):
        span = self.both(d)
        dev = at(self.z, self.x, self.y, 1 - self.c)
        copy = self.links.send(ref.at[span, pl.ds(0, 2 * self.cols)], self.core_in.at[span], dev)
        self.copies[CORE, d] = copy

    def given(self):
        for d in range(4):
            self.links.sent(self.copies[CORE, d])

    def release(self, free_sem):
        z, x, y, c = self.z, self.x, self.y, self.c
        for key, copy in self.copies.items():
            if copy.number in self.links.left:
                self.links.sent(copy)
        near = [at(z, 1 - x, y, c), at(z, x, 1 - y, c), at(z, x, y, 1 - c)]
        for dev in near + [at((z + d) % 4, x, y, c) for d in (1, 2, 3)]:
            pl.semaphore_signal(free_sem, inc=1, device_id=dev, device_id_type=MESH)

    def add(self, span, other):
        here = self.own[span].astype(jnp.float32)
        self.own[span] = (here + other.astype(jnp.float32)).astype(jnp.bfloat16)

    def one(self, d):
        z, x, y, c = self.z, self.x, self.y, self.c
        self.copies[CORE, d].wait_recv()
        self.add((self.both(d), slice(None)), self.core_in[self.both(d), :])
        if d in FIRST_X:
            src = self.own.at[self.both(d), self.side(1 - y)]
            dst, dev = self.one_y.at[FIRST_X.index(d)], at(z, x, 1 - y, c)
        else:
            src = self.own.at[self.strip(self.plane(d) * 2 + 1 - x)]
            dst, dev = self.one_x.at[d - 1], at(z, 1 - x, y, c)
        self.copies[ONE, d] = self.links.send(src, dst, dev)

    def second(self, d):
        z, x, y, c = self.z, self.x, self.y, self.c
        self.copies[ONE, d].wait_recv()
        self.links.sent(self.copies[ONE, d])
        near, far = self.strip(self.plane(d) * 2 + x), self.strip(self.plane(d) * 2 + 1 - x)
        if d in FIRST_X:
            self.add((self.both(d), self.side(y)), self.one_y[FIRST_X.index(d)])
            src, dev = self.own.at[far, self.side(y)], at(z, 1 - x, y, c)
        else:
            self.add((near, slice(None)), self.one_x[d - 1])
            src, dev = self.own.at[near, self.side(1 - y)], at(z, x, 1 - y, c)
        self.copies[TWO, d] = self.links.send(src, self.two.at[d], dev)

    def third(self, d):
        z, x, y, c = self.z, self.x, self.y, self.c
        self.copies[TWO, d].wait_recv()
        near = (self.strip(self.plane(d) * 2 + x), self.side(y))
        self.add(near, self.two[d])
        if d:
            src, dst = self.own.at[near[0], near[1]], self.from_z.at[d - 1]
            self.copies[LAST, d] = self.links.send(src, dst, at(self.plane(d), x, y, c))

    def last(self, out_ref, squares):
        value = self.own[self.strip(self.z * 2 + self.x), self.side(self.y)].astype(jnp.float32)
        for d in (1, 2, 3):
            self.copies[LAST, d].wait_recv()
            value = value + self.from_z[d - 1].astype(jnp.float32)
        out_ref[...] = value
        part = jnp.sum((value * value).reshape(self.rows // 8, 8, self.cols), axis=0)
        for j in range(self.cols // 128):
            squares[...] += part[:, j * 128 : (j + 1) * 128]


def backward_kernel(layers, pairs, coef, w_ref, aux_ref, dh_in, gains_ref, *refs):
    kept = [Kept(*refs[12 * i : 12 * i + 12]) for i in range(layers)]
    refs = refs[12 * layers :]
    weights = [(None,) + refs[4 * i : 4 * i + 4] for i in range(layers)]
    refs = refs[4 * layers :]
    dh = refs[0]
    sums = [(None,) + refs[1 + 4 * i : 5 + 4 * i] for i in range(layers)]
    norm_out, squares = refs[1 + 4 * layers : 3 + 4 * layers]
    rest = refs[3 + 4 * layers :]
    free_sem, send_sem, recv_sem, move_sem = rest[-4:]
    links, moves = Links(send_sem, recv_sem), Moves(move_sem)
    reds = [[None] + [Reduce(*rest[i:24:4], links) for i in range(4)] for _ in range(layers)]
    give_a, give_b, buf_a, buf_b, w_out = rest[24:29]
    hold = Kept(*rest[29:31], None, *rest[31:40])
    drb, turned, dd_ref = rest[40:43]
    ex_refs = [rest[43 + 6 * i : 49 + 6 * i] for i in range(layers)]
    rows, model = dh.shape
    half = rows // 2
    width = model + 128
    hidden = hold.gz.shape[1]
    z, x, y, c = place()
    even = c == 0

    loads = {}

    def load(number, src, dst):
        loads[number] = moves.start(src, dst)

    def need(*numbers):
        for number in numbers:
            moves.wait(loads[number])

    def load_early(layer):
        have = kept[layer]
        load(0, have.xh2, hold.xh2)
        load(1, have.rstd, hold.rstd)
        load(2, weights[layer][DOWN], buf_a)
        load(3, have.n1b, hold.n1b)
        load(4, have.xh1, hold.xh1)
        load(5, have.ob, hold.ob)
        load(6, have.den, hold.den)
        load(7, have.state, hold.state)
        load(8, have.slope, hold.slope)
        load(9, weights[layer][OUT], w_out)

    def load_late(layer):
        load(11, kept[layer].gu, hold.gu)
        load(12, weights[layer][UP], buf_b)

    steps, done, pushed, closed = [], [0], [], {}

    def pump(n):
        while n > 0 and done[0] < len(steps):
            steps[done[0]]()
            done[0] += 1
            n -= 1

    def until(mark):
        pump(mark - done[0])

    def later_stages(i):
        for stage in (1, 2, 3):
            if 0 <= i - stage < len(pushed):
                layer, kind = pushed[i - stage]
                red = reds[layer][kind]
                if stage < 3:
                    for d in (2, 3, 1, 0):
                        steps.append(functools.partial((red.second, red.third)[stage - 1], d))
                else:
                    steps.append(functools.partial(red.last, sums[layer][kind], squares))
                    if layer:
                        steps.append(functools.partial(red.release, free_sem.at[kind]))
                    closed[layer, kind] = len(steps)

    def take(layer, kind):
        if layer < layers - 1:
            until(closed[layer + 1, kind])

    def credit(layer, kind):
        if layer < layers - 1:
            pl.semaphore_wait(free_sem.at[kind], 6)

    def push(layer, kind, ref):
        red = reds[layer][kind]
        pump(len(steps))
        credit(layer, kind)
        for d in (2, 3, 1, 0):
            red.give(ref, d)
        pushed.append((layer, kind))
        for d in (2, 3, 1, 0):
            steps.append(functools.partial(red.one, d))
        later_stages(len(pushed) - 1)

    load(10, kept[layers - 1].gz, hold.gz)
    first_dh = moves.start(dh_in, dh)
    load_early(layers - 1)
    load_late(layers - 1)
    greet()
    squares[...] = jnp.zeros(squares.shape, jnp.float32)
    moves.wait(first_dh)

    cos, sin = aux_ref[:, 0:1], aux_ref[:, 1:2]
    follow, tail, valid = aux_ref[:, 2:3], aux_ref[:, 3:4], aux_ref[:, 4:5]
    low = low_lanes((rows, 128))
    zero = jnp.zeros((rows, 128), jnp.bfloat16)
    ones = jnp.ones((rows, 128), jnp.bfloat16)
    cf, sf = cos * follow, sin * follow
    ct, st = cos * tail, sin * tail

    def turn(ref):
        for i in range(0, model, 256):
            turned[i : i + 256, :] = ref[:, i : i + 256].astype(jnp.float32).T.astype(jnp.bfloat16)

    def choose(first, second):
        return jnp.where(even, first, second), jnp.where(even, second, first)

    def split_rows(block, mine_ref, theirs_ref, span):
        for strip in range(8):
            mine, theirs = choose(
                block[strip * 96 : strip * 96 + 48], block[strip * 96 + 48 : strip * 96 + 96]
            )
            mine_ref[strip * 48 : (strip + 1) * 48, span] = mine
            theirs_ref[strip * 48 : (strip + 1) * 48, span] = theirs

    def q_of(p):
        return buf_a[:rows, p * 128 : (p + 1) * 128]

    def k_of(p):
        return buf_a[:rows, model + p * 128 : model + (p + 1) * 128]

    def v_of(p):
        return buf_a[:rows, 2 * model + p * 128 : 2 * model + (p + 1) * 128]

    def one_layer(layer):
        red = reds[layer]
        down, up, out, qkv = red[DOWN], red[UP], red[OUT], red[QKV]
        ex = Exchange(coef, ex_refs[layer], links, True)

        def norm_back(xh_ref, which):
            gain = gains_ref[layer, 2 * which : 2 * which + 1, :]
            dg = jnp.zeros((8, model), jnp.float32)
            db = jnp.zeros((8, model), jnp.float32)
            for i in range(0, rows, 128):
                dy, xh = dh[i : i + 128, :], xh_ref[i : i + 128, :]
                r = hold.rstd[i : i + 128, which * 64 : which * 64 + 1]
                e = dy * gain
                both = dy * xh
                dx = e - jnp.mean(e, axis=1, keepdims=True)
                dx = r * (dx - xh * jnp.mean(e * xh, axis=1, keepdims=True))
                dg = dg + jnp.sum(both.reshape(16, 8, model), axis=0)
                db = db + jnp.sum(dy.reshape(16, 8, model), axis=0)
                dh[i : i + 128, :] = dx
                drb[i : i + 128, :] = dx.astype(jnp.bfloat16)
                pump(1)
            norm_out[layer, 2 * which : 2 * which + 1, :] = jnp.sum(dg, axis=0, keepdims=True)
            norm_out[layer, 2 * which + 1 : 2 * which + 2, :] = jnp.sum(db, axis=0, keepdims=True)

        norm_out[layer, 4:8, :] = jnp.zeros((4, model), jnp.float32)
        need(0, 1)
        norm_back(hold.xh2, 1)
        turn(drb)
        need(10)
        take(layer, DOWN)
        left = turned[...]
        for strip in range(8):
            block = mm(left, hold.gz[:, strip * 384 : (strip + 1) * 384]).astype(jnp.bfloat16)
            for yy in range(2):
                first = block[yy * 384 : yy * 384 + 192]
                second = block[yy * 384 + 192 : yy * 384 + 384]
                mine, theirs = choose(first, second)
                span = slice(strip * 192, (strip + 1) * 192)
                down.own[span, yy * 384 : (yy + 1) * 384] = mine
                give_a[span, yy * 384 : (yy + 1) * 384] = theirs
            pump(1)
        push(layer, DOWN, give_a)
        need(2, 11)
        low_grad = drb[...]
        for j in range(hidden // 256):
            span = slice(j * 256, (j + 1) * 256)
            t = mm(low_grad, buf_a[:, span]) * hold.gu[:, span].astype(jnp.float32)
            hold.gz[:, span] = t.astype(jnp.bfloat16)
            pump(1)
        du = hold.gz
        load(13, kept[layer].soft, buf_a.at[pl.ds(0, rows), pl.ds(0, 3 * model)])
        need(3)
        turn(hold.n1b)
        take(layer, UP)
        left = turned[...]
        for yy in range(2):
            for target, cc in ((give_b, 1 - c), (up.own, c)):
                for j in range(3):
                    cols = pl.ds(pl.multiple_of((yy * 2 + cc) * 768 + j * 256, 256), 256)
                    block = mm(left, du[:, cols]).astype(jnp.bfloat16)
                    target[:, yy * 768 + j * 256 : yy * 768 + (j + 1) * 256] = block
        push(layer, UP, give_b)
        need(12)
        for j in range(model // 256):
            span = slice(j * 256, (j + 1) * 256)
            dh[:, span] += mm_nt(du[...], buf_b[span, :])
            pump(2)
        load(14, weights[layer][QKV], buf_b.at[:, pl.ds(0, 3 * model)])
        load(15, kept[layer].acts, hold.acts)
        need(4)
        norm_back(hold.xh1, 0)
        need(5)
        turn(hold.ob)
        take(layer, OUT)
        down.given()
        left = turned[...]
        for j in range(model // 256):
            span = slice(j * 256, (j + 1) * 256)
            block = mm(left, drb[:, span]).astype(jnp.bfloat16)
            split_rows(block, out.own, give_a, span)
        push(layer, OUT, give_a)
        need(9)
        dob_ref = du.at[:, pl.ds(0, model)]
        dn_ref = du.at[:, pl.ds(model, model)]
        dob_ref[...] = mm_nt(drb[...], w_out[...]).astype(jnp.bfloat16)
        pump(2)

        need(13, 6, 7, 8)
        grad, state_ref = hold.gu, hold.state
        keep_k, keep_v = hold.xh2, hold.xh1
        den = hold.den[...]
        inv = 1.0 / jnp.maximum(den, 1.0)
        dots = jnp.zeros((rows, 128), jnp.float32)
        for p in range(pairs):
            dob = dob_ref[:, pair_cols(p)].astype(jnp.float32)
            dn_ref[:, pair_cols(p)] = (dob * spread(inv, p)).astype(jnp.bfloat16)
            both = dob * hold.ob[:, pair_cols(p)].astype(jnp.float32)
            first = jnp.sum(jnp.where(low, both, 0.0), axis=1, keepdims=True)
            second = jnp.sum(jnp.where(low, 0.0, both), axis=1, keepdims=True)
            dots = dots + jnp.where(lane_is((rows, 128), 2 * p), first, 0.0)
            dots = dots + jnp.where(lane_is((rows, 128), 2 * p + 1), second, 0.0)
        dden = jnp.where(den > 1.0, -dots * inv, 0.0)
        dd_ref[...] = dden
        dden_low = dden.astype(jnp.bfloat16)
        extras = [None, None]
        for p in range(pairs):
            qp = q_of(p).astype(jnp.float32)
            rhs = jnp.concatenate([dn_ref[:, pair_cols(p)], dden_low], axis=1)
            for kind, angle in enumerate((cf, sf)):
                block = mm_tn((qp * angle).astype(jnp.bfloat16), rhs)
                extras[kind] = pack_state(ex.mine, p, kind, block, extras[kind])
        for kind in range(2):
            store_extra(ex.mine, kind, extras[kind], width)
        ex.scatter()

        def inner(p):
            qp, kp, vp = q_of(p), k_of(p), v_of(p)
            dob, dnp = dob_ref[:, pair_cols(p)], dn_ref[:, pair_cols(p)]
            q_t = qp.astype(jnp.float32).T.astype(jnp.bfloat16)
            dn_t = dnp.astype(jnp.float32).T.astype(jnp.bfloat16)
            dq_parts, dk_parts, dv_parts = [], [], []
            for e in range(2):
                h = 2 * p + e
                mask = low if e == 0 else ~low
                span = slice(e * HD, (e + 1) * HD)
                qh = jnp.where(mask, qp, zero)
                doh = jnp.where(mask, dob, zero)
                scale, shift = inv[:, h : h + 1], dd_ref[:, h : h + 1]

                def tile(at_rows, at_cols):
                    weight = w_ref[at_rows, at_cols]
                    s = (mm_nt(qh[at_rows], kp[at_cols]) * weight).astype(jnp.bfloat16)
                    t = mm_nt(doh[at_rows], vp[at_cols])
                    ds = (t * scale[at_rows] + shift[at_rows]).astype(jnp.bfloat16)
                    g = (ds.astype(jnp.float32) * weight).astype(jnp.bfloat16)
                    return s, g

                above, below, every = slice(0, half), slice(half, rows), slice(0, rows)
                s_top, g_top = tile(above, above)
                s_low, g_low = tile(below, every)
                dq_parts.append(jnp.concatenate([mm(g_top, kp[:half]), mm(g_low, kp)], axis=0))

                def across(flat, top, bottom):
                    whole = mm(flat[span, half:], bottom)
                    first = whole[:, :half] + mm(flat[span, :half], top)
                    return jnp.concatenate([first, whole[:, half:]], axis=1)

                dk_parts.append(across(q_t, g_top, g_low))
                dv_parts.append(across(dn_t, s_top, s_low))
            base = slice(p * 128, (p + 1) * 128)
            dq = jnp.where(low, dq_parts[0], dq_parts[1])
            right = jnp.concatenate([dnp, dd_ref[...].astype(jnp.bfloat16)], axis=1)
            dq += cf * mm_nt(right, unpack_state(state_ref, p, 0, width))
            dq += sf * mm_nt(right, unpack_state(state_ref, p, 1, width))
            slope = hold.slope[:, base].astype(jnp.float32)
            grad[:, base] = (dq * slope).astype(jnp.bfloat16)
            keep_k[:, base] = jnp.concatenate(dk_parts, axis=0).T
            keep_v[:, base] = jnp.concatenate(dv_parts, axis=0).T

        for p in range(pairs):
            inner(p)
            if p == 1:
                ex.across()
            if p == 3:
                ex.gather()
            pump(3)
        ex.finish()
        for p in range(pairs):
            base = p * 128
            dsc, dss = unpack_state(ex.result, p, 0, width), unpack_state(ex.result, p, 1, width)
            right = jnp.concatenate([v_of(p), ones], axis=1)
            dk = keep_k[:, base : base + 128] + ct * mm_nt(right, dsc) + st * mm_nt(right, dss)
            kp = k_of(p)
            dv = ct * mm(kp, dsc[:, :128]) + st * mm(kp, dss[:, :128])
            dv = keep_v[:, base : base + 128] + dv
            slope = hold.slope[:, model + base : model + base + 128].astype(jnp.float32)
            grad[:, model + base : model + base + 128] = (dk * valid * slope).astype(jnp.bfloat16)
            grad[:, 2 * model + base : 2 * model + base + 128] = dv.astype(jnp.bfloat16)
        need(15)
        turn(hold.acts)
        if layer:
            load_early(layer - 1)
        take(layer, QKV)
        left = turned[...]
        for j in range(3 * model // 256):
            span = slice(j * 256, (j + 1) * 256)
            block = mm(left, grad[:, span]).astype(jnp.bfloat16)
            split_rows(block, qkv.own, hold.gz, span)
        push(layer, QKV, hold.gz)
        up.given()
        out.given()
        need(14)
        for j in range(model // 256):
            span = slice(j * 256, (j + 1) * 256)
            dh[:, span] += mm_nt(grad[:, : 3 * model], buf_b[span, : 3 * model])
            pump(2)
        qkv.given()
        if layer:
            load(10, kept[layer - 1].gz, hold.gz)
            load_late(layer - 1)

    for layer in reversed(range(layers)):
        one_layer(layer)
    for i in range(len(pushed), len(pushed) + 3):
        later_stages(i)
    pump(len(steps))
    moves.finish()
    links.finish()


def backward(number, coef, weights_map, aux, dh, held, dims):
    rows, model = dh.shape
    layers = len(held)
    gains = jnp.stack([h[0] for h in held])
    kept = held[0][2]
    hidden = kept.gz.shape[1]
    width = model + 128
    low, wide = jnp.bfloat16, jnp.float32
    vmem = pl.BlockSpec(memory_space=pltpu.VMEM)
    anywhere = pl.BlockSpec(memory_space=pl.ANY)
    sizes = dims[1:]
    scratch = [pltpu.VMEM((8 * r, 2 * w), low) for r, w in sizes] * 2
    scratch += [pltpu.VMEM((2, 2 * r, w), low) for r, w in sizes]
    scratch += [pltpu.VMEM((2, r, 2 * w), low) for r, w in sizes]
    scratch += [pltpu.VMEM((4, r, w), low) for r, w in sizes]
    scratch += [pltpu.VMEM((3, r, w), low) for r, w in sizes]
    for k in (DOWN, UP):
        scratch.append(pltpu.VMEM((8 * dims[k][0], 2 * dims[k][1]), low))
    scratch += [pltpu.VMEM((model, hidden), low)] * 2
    scratch.append(pltpu.VMEM((model, model), low))
    scratch += [pltpu.VMEM(a.shape, a.dtype) for a in kept[:2] + kept[3:]]
    scratch += [pltpu.VMEM((rows, model), low), pltpu.VMEM((model, rows), low)]
    scratch += [pltpu.VMEM((rows, 128), wide)]
    scratch += exchange_scratch(width) * layers
    scratch += [pltpu.SemaphoreType.REGULAR((5,))]
    scratch += [pltpu.SemaphoreType.DMA((layers * 80,))] * 2
    scratch += [pltpu.SemaphoreType.DMA((layers * 20,))]
    outs = pl.pallas_call(
        functools.partial(backward_kernel, layers, model // 128),
        out_shape=[jax.ShapeDtypeStruct((rows, model), wide)]
        + [jax.ShapeDtypeStruct(s, wide) for s in sizes] * layers
        + [
            jax.ShapeDtypeStruct((layers, 8, model), wide),
            jax.ShapeDtypeStruct((8, 128), wide),
        ],
        in_specs=[pl.BlockSpec(memory_space=pltpu.SMEM)]
        + [vmem, vmem, anywhere, vmem]
        + [anywhere] * (16 * layers),
        out_specs=[vmem] * (3 + 4 * layers),
        scratch_shapes=scratch,
        compiler_params=pltpu.CompilerParams(
            collective_id=number, has_side_effects=True, vmem_limit_bytes=63 * 2**20
        ),
        name="backward_layers",
    )(
        coef, weights_map, aux, dh, gains,
        *[a for h in held for a in h[2]],
        *[a for h in held for a in h[1]],
    )
    sums = [[None, *outs[1 + 4 * i : 5 + 4 * i]] for i in range(layers)]
    return outs[0], sums, outs[-2], outs[-1]


def stream_meta(lengths, row_ids):
    seq_count = lengths.shape[0]
    seq_ends = jnp.cumsum(lengths, dtype=jnp.int32)
    seq_starts = seq_ends - lengths
    begun = seq_starts[None, :] <= row_ids[:, None]
    seg_raw = jnp.sum(begun.astype(jnp.int32), axis=1, dtype=jnp.int32) - 1
    seg_start = jnp.max(jnp.where(begun, seq_starts[None, :], 0), axis=1)
    inside = row_ids < seq_ends[seq_count - 1]
    seg_ids = jnp.where(inside, seg_raw, seq_count)
    offsets = jnp.where(inside, row_ids - seg_start, 0).astype(jnp.float32)
    angles = offsets * (0.5 * math.pi / LONGEST)
    return (seg_ids, jnp.cos(angles), jnp.sin(angles), inside.astype(jnp.float32))


def adam_step(weight, first_old, second_old, gradient, factor, step_rate, decay_coef):
    clipped = gradient * factor
    first_new = beta_one * first_old + (1.0 - beta_one) * clipped
    second_new = beta_two * second_old + (1.0 - beta_two) * clipped * clipped
    first_hat = first_new / (1.0 - beta_one**step_fixed)
    second_hat = second_new / (1.0 - beta_two**step_fixed)
    weight_new = weight - step_rate * (
        first_hat / (jnp.sqrt(second_hat) + adam_eps) + decay_coef * weight
    )
    return (weight_new, first_new, second_new)


def other_core(array):
    return lax.ppermute(array, "head", [(0, 1), (1, 0), (2, 3), (3, 2)])


def weight_pieces(w_qkv, w_out, w_up, w_down, norm_params):
    first = lax.axis_index("head") % 2 == 0
    low = [a.astype(jnp.bfloat16) for a in (w_qkv, w_out)]
    halves = [(a[:, : a.shape[1] // 2], a[:, a.shape[1] // 2 :]) for a in low]
    keep = [jnp.where(first, a, b) for a, b in halves]
    give = [jnp.where(first, b, a) for a, b in halves]
    wide = other_core(jnp.concatenate(give, axis=2))
    got = jnp.split(wide, (keep[0].shape[2],), axis=2)
    pieces = [
        jnp.where(first, jnp.concatenate([a, b], axis=2), jnp.concatenate([b, a], axis=2))
        for a, b in zip(keep, got)
    ]
    pieces.append(w_up.astype(jnp.bfloat16))
    pieces.append(w_down.astype(jnp.bfloat16).transpose(0, 2, 1))
    layers, _, part = norm_params.shape
    norm = norm_params.astype(jnp.bfloat16).reshape(layers, part)
    return [jnp.pad(norm, ((0, 16 - layers), (0, 128 - part)))] + pieces


def exchange_plan(seg_last, seg_before, seg_plane, reverse):
    dp = lax.axis_index("dp")
    z = dp // 2
    last = lax.dynamic_slice(seg_last, (z * 8,), (8,))
    before = lax.dynamic_slice(seg_before, (z * 8,), (8,))
    order = jnp.arange(8)
    inside = (before[:, None] == last[None, :]) & (order[:, None] > order[None, :])
    ends = seg_last[7::8]
    planes = jnp.arange(4)
    to_end = last == ends[z]
    back = (before[:, None] == ends[None, :]) & (planes[None, :] < z)
    coef = jnp.zeros((16, 16), jnp.float32)
    shift = jnp.arange(1, 4)
    if reverse:
        coef = coef.at[:8, :8].set(inside.T.astype(jnp.float32))
        source = (z - shift) % 4
        coef = coef.at[:8, 8:11].set((to_end[:, None] & (source > z)[None, :]).astype(jnp.float32))
        target = (z + shift) % 4
        coef = coef.at[9:12, :8].set(back[:, target].T.astype(jnp.float32))
    else:
        coef = coef.at[:8, :8].set(inside.astype(jnp.float32))
        source = (z - shift) % 4
        coef = coef.at[:8, 8:11].set(back[:, source].astype(jnp.float32))
        coef = coef.at[9:12, :8].set(jnp.broadcast_to(to_end.astype(jnp.float32), (3, 8)))
    return coef


class LocalPlan:
    def __init__(self, lengths, rows):
        me = lax.axis_index("dp") * 4 + lax.axis_index("head")
        first_row = me * rows
        seg, cos, sin, valid = stream_meta(lengths, first_row + jnp.arange(rows, dtype=jnp.int32))
        starts = jnp.arange(32, dtype=jnp.int32) * rows
        before = stream_meta(lengths, starts - 1)[0]
        last = stream_meta(lengths, starts + rows - 1)[0]
        follow = (seg == before[me]).astype(jnp.float32)
        tail = (seg == last[me]).astype(jnp.float32)
        place_ids = jnp.arange(rows)
        allowed = (seg[:, None] == seg[None, :]) & (place_ids[None, :] <= place_ids[:, None])
        close = cos[:, None] * cos[None, :] + sin[:, None] * sin[None, :]
        self.valid = valid
        self.weights = jnp.where(allowed, close, 0.0)
        zero = jnp.zeros_like(cos)
        self.aux = jnp.stack([cos, sin, follow, tail, valid, zero, zero, zero], axis=1)
        self.ahead = exchange_plan(last, before, None, False)
        self.behind = exchange_plan(last, before, None, True)


def total_kernel(mine_ref, out_ref, sums, from_z, from_plane, send_sem, recv_sem):
    links = Links(send_sem, recv_sem)
    greet()
    devices = partners()
    copies = [links.send(mine_ref, from_z.at[i], devices[i]) for i in range(3)]
    total = mine_ref[...]
    for i in range(3):
        copies[i].wait_recv()
        total = total + from_z[i]
    sums[...] = total
    copies = [links.send(sums, from_plane.at[i], devices[3 + i]) for i in range(7)]
    for i in range(7):
        copies[i].wait_recv()
        total = total + from_plane[i]
    out_ref[...] = total
    links.finish()


def total_over_devices(number, mine):
    vmem = pl.BlockSpec(memory_space=pltpu.VMEM)
    return pl.pallas_call(
        total_kernel,
        out_shape=jax.ShapeDtypeStruct(mine.shape, mine.dtype),
        in_specs=[vmem],
        out_specs=vmem,
        scratch_shapes=[
            pltpu.VMEM(mine.shape, mine.dtype),
            pltpu.VMEM((3,) + mine.shape, mine.dtype),
            pltpu.VMEM((7,) + mine.shape, mine.dtype),
            pltpu.SemaphoreType.DMA((10,)),
            pltpu.SemaphoreType.DMA((10,)),
        ],
        compiler_params=pltpu.CompilerParams(
            collective_id=number, has_side_effects=True, vmem_limit_bytes=32 * 2**20
        ),
        name="total_over_devices",
    )(mine)


def own_columns(sums):
    first = lax.axis_index("head") % 2 == 0
    halves = [(a[..., : a.shape[2] // 2], a[..., a.shape[2] // 2 :]) for a in sums]
    keep = [jnp.where(first, a, b) for a, b in halves]
    give = [jnp.where(first, b, a) for a, b in halves]
    wide = other_core(jnp.concatenate(give, axis=2))
    got = jnp.split(wide, (keep[0].shape[2],), axis=2)
    return [
        jnp.where(first, jnp.concatenate([a, b], axis=1), jnp.concatenate([b, a], axis=1))
        for a, b in zip(keep, got)
    ]


def near_step(inputs, cotangent, lengths, w_qkv, w_out, w_up, w_down, norm_params):
    rows, model = inputs.shape
    layers, _, part = norm_params.shape
    plan = LocalPlan(lengths, rows)
    pieces = weight_pieces(w_qkv, w_out, w_up, w_down, norm_params)
    dims = [p.shape[-2:] for p in pieces]
    hidden, held = forward(0, plan.ahead, inputs, plan.weights, plan.aux, pieces)
    grad = cotangent.astype(jnp.float32)
    grad, sums, norms, squares = backward(
        1, plan.behind, plan.weights, plan.aux, grad, held, dims
    )
    norms = norms[:, :4].reshape(4 * layers, model)
    squares = jnp.pad(squares, ((0, 0), (0, model - 128)))
    totals = total_over_devices(2, jnp.concatenate([norms, squares], axis=0))
    norm_sum, squares = totals[: 4 * layers], totals[4 * layers :]
    squares = jnp.sum(squares) + jnp.sum(norm_sum * norm_sum)
    start = (0, lax.axis_index("head"), lax.axis_index("dp") * part)
    norm_sum = lax.dynamic_slice(norm_sum.reshape(layers, 4, model), start, (layers, 1, part))
    stacked = [None] + [jnp.stack([s[k] for s in sums]) for k in MATRICES]
    d_qkv, d_out = own_columns([stacked[QKV], stacked[OUT]])
    whole = [d_qkv, d_out, stacked[UP], stacked[DOWN].transpose(0, 2, 1)]
    return hidden, grad, whole, norm_sum, squares


def layer_norm(inputs_row, gain_row, shift_row):
    mean_row = jnp.mean(inputs_row, axis=-1, keepdims=True)
    centered = inputs_row - mean_row
    variance = jnp.mean(centered * centered, axis=-1, keepdims=True)
    return centered * lax.rsqrt(variance + norm_eps) * gain_row + shift_row


def gelu_exact(inner_pre):
    return jax.nn.gelu(inner_pre, approximate=False)


def contract_rows(left, right):
    return lax.dot_general(
        left, right, (((0,), (0,)), ((), ())), preferred_element_type=jnp.float32
    )


def contract_cols(left, right):
    return lax.dot_general(
        left, right, (((1,), (1,)), ((), ())), preferred_element_type=jnp.float32
    )


def block_attention(queries, key_rows, value_rows, weights, aux):
    cos, sin, tail = aux[:, 0], aux[:, 1], aux[:, 3]
    raw = jnp.einsum("ihe,jhe->hij", queries, key_rows, preferred_element_type=jnp.float32)
    scores = (raw * weights[None]).astype(jnp.bfloat16)
    num = jnp.einsum("hij,jhe->ihe", scores, value_rows, preferred_element_type=jnp.float32)
    den = jnp.transpose(jnp.sum(scores.astype(jnp.float32), axis=2))
    out = []
    for angle in (cos, sin):
        turned = key_rows.astype(jnp.float32) * (angle * tail)[:, None, None]
        out.append(
            jnp.einsum(
                "jhe,jhf->hef", turned, value_rows.astype(jnp.float32), precision=exact_mode
            )
        )
        out.append(jnp.sum(turned, axis=0))
    return num, den, tuple(out)


def finish_rows(queries, num, den, state, aux):
    cos, sin, follow = aux[:, 0], aux[:, 1], aux[:, 2]
    for angle, kv, ks in ((cos, state[0], state[1]), (sin, state[2], state[3])):
        turned = queries.astype(jnp.float32) * (angle * follow)[:, None, None]
        num = num + jnp.einsum("ihe,hef->ihf", turned, kv, precision=exact_mode)
        den = den + jnp.einsum("ihe,he->ih", turned, ks, precision=exact_mode)
    return num / jnp.maximum(den, 1.0)[:, :, None]


class WidePlan:
    def __init__(self, lengths, rows):
        parts = lax.axis_size("dp") * lax.axis_size("head")
        me = lax.axis_index("dp") * lax.axis_size("head") + lax.axis_index("head")
        seg, cos, sin, valid = stream_meta(
            lengths, me * rows + jnp.arange(rows, dtype=jnp.int32)
        )
        starts = jnp.arange(parts, dtype=jnp.int32) * rows
        before = stream_meta(lengths, starts - 1)[0]
        last = stream_meta(lengths, starts + rows - 1)[0]
        follow = (seg == before[me]).astype(jnp.float32)
        tail = (seg == last[me]).astype(jnp.float32)
        place_ids = jnp.arange(rows)
        allowed = (seg[:, None] == seg[None, :]) & (place_ids[None, :] <= place_ids[:, None])
        close = cos[:, None] * cos[None, :] + sin[:, None] * sin[None, :]
        self.valid = valid
        self.weights = jnp.where(allowed, close, 0.0)
        self.aux = jnp.stack([cos, sin, follow, tail, valid], axis=1)
        devices = jnp.arange(parts)
        self.ahead = ((last == before[me]) & (devices < me)).astype(jnp.float32)
        self.behind = ((before == last[me]) & (devices > me)).astype(jnp.float32)

    def masked(self, state, coef):
        def one(a):
            everything = lax.all_gather(a.astype(jnp.bfloat16), ("dp", "head"))
            return jnp.einsum(
                "d,d...->...",
                coef.astype(jnp.bfloat16),
                everything,
                preferred_element_type=jnp.float32,
            )

        return jax.tree.map(one, state)

    def attend(self, q, k, v):
        rows, model = q.shape
        split = lambda a: a.reshape(rows, HEADS, model // HEADS)
        local = lambda *a: block_attention(*a, self.weights, self.aux)
        (num, den, state), pull = jax.vjp(local, split(q), split(k), split(v))
        state = self.masked(state, self.ahead)
        finish = lambda *a: finish_rows(*a, self.aux)
        out, finish_pull = jax.vjp(finish, split(q), num, den, state)
        return out.astype(jnp.bfloat16).reshape(rows, model), (pull, finish_pull)

    def attend_back(self, kept, dob):
        pull, finish_pull = kept
        rows, model = dob.shape
        grad = dob.astype(jnp.float32).reshape(rows, HEADS, model // HEADS)
        dq_one, dnum, dden, dstate = finish_pull(grad)
        dstate = self.masked(dstate, self.behind)
        dq, dk, dv = pull((dnum, dden, dstate))
        dq = dq.astype(jnp.float32) + dq_one.astype(jnp.float32)
        dk = dk.astype(jnp.float32) * self.valid[:, None, None]
        out = [a.reshape(rows, model).astype(jnp.bfloat16) for a in (dq, dk, dv)]
        return jnp.concatenate(out, axis=1)


def wide_gather(w_qkv, w_out, w_up, w_down, norm_params):
    fulls = []
    for a in (w_qkv, w_out, w_up, w_down):
        part = lax.all_gather(a.astype(jnp.bfloat16), "dp", axis=1, tiled=True)
        fulls.append(lax.all_gather(part, "head", axis=2, tiled=True))
    norm = lax.all_gather(norm_params.astype(jnp.bfloat16), "dp", axis=2, tiled=True)
    return fulls, lax.all_gather(norm, "head", axis=1, tiled=True)


def wide_reduce(grads, norm_grad):
    def one(a):
        part = lax.psum_scatter(a, "head", scatter_dimension=1, tiled=True)
        part = lax.psum_scatter(part.astype(jnp.float32), "dp", scatter_dimension=0, tiled=True)
        return part

    whole = [jnp.stack([one(layer[i]) for layer in grads]) for i in range(len(grads[0]))]
    part = lax.psum_scatter(norm_grad, "head", scatter_dimension=1, tiled=True)
    norm = lax.psum_scatter(part, "dp", scatter_dimension=2, tiled=True)
    squares = sum([jnp.sum(a * a) for a in whole + [norm]])
    return whole, norm, lax.psum(squares, ("dp", "head"))


def wide_step(inputs, cotangent, lengths, w_qkv, w_out, w_up, w_down, norm_params):
    rows, model = inputs.shape
    layers = w_qkv.shape[0]
    plan = WidePlan(lengths, rows)
    fulls, norm_full = wide_gather(w_qkv, w_out, w_up, w_down, norm_params)
    norm_full = norm_full.astype(jnp.float32)
    hidden = inputs.astype(jnp.float32)
    kept = []
    for layer in range(layers):
        qkv_w, out_w, up_w, down_w = (a[layer] for a in fulls)
        gains = norm_full[layer]
        acts = hidden.astype(jnp.bfloat16)
        mixed = jnp.dot(acts, qkv_w, preferred_element_type=jnp.float32)
        soft = jax.nn.softplus(mixed[:, : 2 * model]).astype(jnp.bfloat16)
        q = soft[:, :model]
        k = soft[:, model:] * plan.valid[:, None].astype(jnp.bfloat16)
        v = mixed[:, 2 * model :].astype(jnp.bfloat16)
        attended, attend_kept = plan.attend(q, k, v)
        first_in = hidden + jnp.dot(attended, out_w, preferred_element_type=jnp.float32)
        first_out = layer_norm(first_in, gains[0], gains[1])
        first_low = first_out.astype(jnp.bfloat16)
        inner = jnp.dot(first_low, up_w, preferred_element_type=jnp.float32)
        act = gelu_exact(inner).astype(jnp.bfloat16)
        second_in = first_out + jnp.dot(act, down_w, preferred_element_type=jnp.float32)
        kept.append((acts, mixed, attend_kept, attended, first_in, first_low, inner, act, second_in))
        hidden = layer_norm(second_in, gains[2], gains[3])
    grad_hidden = cotangent.astype(jnp.float32)
    grads = [None] * layers
    norm_grads = [None] * layers
    for layer in reversed(range(layers)):
        acts, mixed, attend_kept, attended, first_in, first_low, inner, act, second_in = kept[layer]
        qkv_w, out_w, up_w, down_w = (a[layer] for a in fulls)
        gains = norm_full[layer]
        _, pull_two = jax.vjp(layer_norm, second_in, gains[2], gains[3])
        grad_second, dgain_two, dshift_two = pull_two(grad_hidden)
        branch_two = grad_second.astype(jnp.bfloat16)
        dw_down = contract_rows(act, branch_two).astype(jnp.bfloat16)
        grad_act = contract_cols(branch_two, down_w)
        _, gelu_pull = jax.vjp(gelu_exact, inner)
        grad_inner = gelu_pull(grad_act)[0].astype(jnp.bfloat16)
        dw_up = contract_rows(first_low, grad_inner).astype(jnp.bfloat16)
        grad_first = grad_second + contract_cols(grad_inner, up_w)
        _, pull_one = jax.vjp(layer_norm, first_in, gains[0], gains[1])
        grad_first_in, dgain_one, dshift_one = pull_one(grad_first)
        branch = grad_first_in.astype(jnp.bfloat16)
        dw_out = contract_rows(attended, branch).astype(jnp.bfloat16)
        dob = contract_cols(branch, out_w).astype(jnp.bfloat16)
        grad_mixed = plan.attend_back(attend_kept, dob)
        slope = jax.nn.sigmoid(mixed[:, : 2 * model])
        grad_soft = (grad_mixed[:, : 2 * model].astype(jnp.float32) * slope).astype(jnp.bfloat16)
        grad_pre = jnp.concatenate([grad_soft, grad_mixed[:, 2 * model :]], axis=1)
        dw_qkv = contract_rows(acts, grad_pre).astype(jnp.bfloat16)
        grad_hidden = grad_first_in + contract_cols(grad_pre, qkv_w)
        grads[layer] = (dw_qkv, dw_out, dw_up, dw_down)
        norm_grads[layer] = jnp.stack([dgain_one, dshift_one, dgain_two, dshift_two])
    whole, norm_sum, squares = wide_reduce(grads, jnp.stack(norm_grads))
    return hidden, grad_hidden, whole, norm_sum, squares


def body(
    inputs, cotangent, lengths,
    w_qkv, m_qkv, v_qkv, w_out, m_out, v_out, w_up, m_up, v_up, w_down, m_down, v_down,
    norm_params, m_norm, v_norm,
):
    rows = inputs.shape[0]
    near = lax.axis_size("dp") == 8 and lax.axis_size("head") == 4 and rows == 512
    hidden, grad_hidden, whole, norm_sum, squares = (near_step if near else wide_step)(
        inputs, cotangent, lengths, w_qkv, w_out, w_up, w_down, norm_params
    )
    grad_norm = jnp.sqrt(squares)
    factor = clip_limit / jnp.maximum(grad_norm, clip_limit)
    new_qkv = adam_step(w_qkv, m_qkv, v_qkv, whole[0], factor, rate_matrix, decay_rate)
    new_out = adam_step(w_out, m_out, v_out, whole[1], factor, rate_outproj, decay_rate)
    new_up = adam_step(w_up, m_up, v_up, whole[2], factor, rate_matrix, decay_rate)
    new_down = adam_step(w_down, m_down, v_down, whole[3], factor, rate_matrix, decay_rate)
    new_norm = adam_step(norm_params, m_norm, v_norm, norm_sum, factor, rate_norm, 0.0)
    return (
        (hidden, grad_hidden, grad_norm.reshape(1))
        + new_qkv + new_out + new_up + new_down + new_norm
    )


def solution(mesh):
    rows = P(("dp", "head"), None)
    weight = P(None, "dp", "head")
    norm = P(None, "head", "dp")
    in_specs = (rows, rows, P()) + (weight,) * 12 + (norm,) * 3
    out_specs = (rows, rows, P()) + (weight,) * 12 + (norm,) * 3
    return jax.shard_map(body, mesh=mesh, in_specs=in_specs, out_specs=out_specs, check_vma=False)
```

time: 604 us -> 411 us (0.68)
  matrix products: 136 us -> 0 us
  local copies, waits for them, and re-layouts: 36.4 us -> 15.7 us
  other arithmetic: 48.5 us -> 29 us
  Pallas kernels: 374 us -> 358 us
    dot_general x24 -> x0, matrix products: 136 us -> none  [the longest x8 43 us: contract_cols(): lax.dot_general(left, right, (((1,), (1,)), ((), ())), preferred_element_...]
    pallas_call x6 -> x3, Pallas kernels: 374 us -> 358 us  [the longest x1 177 us: backward(): pl.pallas_call(functools.partial(backward_kernel, layers, model // 128),...]
    unnamed x137 -> x56, local copies, waits for them, and re-layouts: 17.5 us -> 4.28 us
    select_n x12 -> x6, other arithmetic: 12.5 us -> 4.01 us  [the longest x2 1.56 us: weight_pieces(): jnp.where(first, jnp.concatenate([a, b], axis=2), jnp.concatenate([b, a],...]
    reduce_sum x11 -> x1, other arithmetic: 6.81 us -> 0.61 us  [near_step(): squares = jnp.sum(squares) + jnp.sum(norm_sum * norm_sum)]
  transfers between devices with their start and end apart: 4 -> 2, of which waited for: 0 -> 0; matrix products, arithmetic and copies ran while one was open for 9% -> 7% of each run, Pallas kernels for 0% -> 0%
where the time goes in v2:
time: 411 us; the launch traced here: 407 us
  Pallas kernels  358 us (87%)
  other arithmetic  29 us (7%)
  local copies, waits for them, and re-layouts  15.7 us (4%)
    pallas_call x1, Pallas kernels, backward(): pl.pallas_call(functools.partial(backward_kernel, layers, model // 128),...  177 us
    pallas_call x1, Pallas kernels, forward(): pl.pallas_call(functools.partial(forward_kernel, layers, model // 128), o...  166 us
    pallas_call x1, Pallas kernels, total_over_devices(): pl.pallas_call(total_kernel, out_shape=jax.ShapeDtypeStruct(mine.shape, m...  14.6 us
  transfers between devices with their start and end apart: 2, of which 0 were waited for; matrix products, arithmetic and copies ran while one was open for 7% of the time, Pallas kernels for 0%

profile of v2, /device:TPU:0, one launch (start us, length us, event | category | flops | bytes accessed | tf_op | source)
XLA Modules:
  0.0 407.1 jit_solution(12767218089713577791)
XLA Ops:
  0.7 1.0 convert_element_type.115
  1.7 1.1 convert_element_type.114
  13.5 2.0 dynamic-slice_select_fusion
  15.5 1.9 scatter.40
  17.3 2.0 bitcast_select_fusion
  19.4 1.9 scatter.36
  21.2 1.9 compare_convert_fusion.1
  23.2 0.8 copy.52.aux_ref
  24.8 1.3 convert_element_type.121.dh_in
  27.4 1.3 add_select_fusion.w_ref
  29.5 0.8 maximum_select_fusion.1.refs_1_
  31.2 166.2 %forward_layers.1 = (f32[512,768]{1,0:T(8,128)}, f32[2,8,768]{2,1,0:T(8,128)}, bf16[768,2304]{1,0:T(8,128)(2,1)}, bf16[768,768]{1,0:T(8,128)(2,1)}, bf16[768,307...) custom-call(f32[16,16]{1,0:T(8,128)} %copy-done.20, ...), custom_call_target="tpu_custom_call" | custom-call | tf_op jit(solution)/shard_map/forward_layers/pallas_call | solution.py:598
  197.4 176.7 %backward_layers.1 = (f32[512,768]{1,0:T(8,128)}, f32[48,1152]{1,0:T(8,128)}, f32[48,384]{1,0:T(8,128)}, f32[96,768]{1,0:T(8,128)}, f32[192,384]{1,0:T(8,128)}, ...) custom-call(f32[16,16]{1,0:T(8,128)} %copy-done.21, ...), custom_call_target="tpu_custom_call" | custom-call | tf_op jit(solution)/shard_map/backward_layers/pallas_call | solution.py:1079
  374.2 0.9 slice.184
  375.8 14.6 %total_over_devices.1 = f32[16,768]{1,0:T(8,128)S(1)} custom-call(f32[16,768]{1,0:T(8,128)S(1)} %select_maximum_fusion.mine_ref), custom_call_target="tpu_custom_call" | custom-call | tf_op jit(solution)/shard_map/total_over_devices/pallas_call | solution.py:1222
  392.4 1.1 fusion.13
  393.5 1.3 broadcast_select_fusion
  395.4 1.5 multiply_subtract_fusion
  397.7 1.5 multiply_subtract_fusion.1
  399.3 0.9 multiply_subtract_fusion.3
  400.7 1.4 multiply_subtract_fusion.2
  402.7 1.1 copy.60
  403.8 0.8 copy-done.5
  404.6 1.1 copy.61
  (119 shorter events, 17.9 us)
Async XLA Ops:
  0.7 3.7 copy-start.26
  0.7 2.9 copy-start.25
  0.7 4.4 %copy-start.22 = (f32[2,1,96]{2,1,0:T(1,128)S(1)}, f32[2,1,96]{2,1,0:T(1,128)}, u32[]{:S(2)}) copy-start(f32[2,1,96]{2,1,0:T(1,128)} %param.45) | copy-start | bytes 2308
  0.7 23.4 %copy-start.1 = (f32[2,96,768]{2,1,0:T(8,128)S(1)}, f32[2,96,768]{2,1,0:T(8,128)}, u32[]{:S(2)}) copy-start(f32[2,96,768]{2,1,0:T(8,128)} %param.39) | copy-start | bytes 1769476
  1.7 23.1 %copy-start.7 = (bf16[512,768]{1,0:T(8,128)(2,1)S(1)}, bf16[512,768]{1,0:T(8,128)(2,1)}, u32[]{:S(2)}) copy-start(bf16[512,768]{1,0:T(8,128)(2,1)} %param.31) | copy-start | bytes 2359300
  3.0 26.5 %collective-permute-start = (bf16[2,48,768]{2,1,0:T(8,128)(2,1)S(1)}, bf16[2,48,768]{2,1,0:T(8,128)(2,1)S(1)}, u32[]{:S(2)}, u32[]{:S(2)}) collective-permute-start(bf16[2,48,768]{2,1,0:T(8,128)(2,1)S(1)} %pad_maximum_fusion.2), channel_id=1, source_target_pairs={{0,1},{1,0},{2,3},{3,2},{4,5},{5,4},{6,7},{7,6},{8,9},{9,8},{10,11... | collective-permute-start | bytes 442376 | tf_op jit(solution)/shard_map/ppermute | solution.py:1132
  24.8 3.9 copy-start
  26.9 170.5 %copy-start.21 = (f32[16,16]{1,0:T(8,128)}, f32[16,16]{1,0:T(8,128)S(1)}, u32[]{:S(2)}) copy-start(f32[16,16]{1,0:T(8,128)S(1)} %scatter.41.coef) | copy-start | bytes 3076
  27.4 3.7 copy-start.20
  374.2 21.2 %copy-start.8 = (f32[2,384,192]{1,2,0:T(8,128)S(1)}, f32[2,384,192]{1,2,0:T(8,128)}, u32[]{:S(2)}) copy-start(f32[2,384,192]{1,2,0:T(8,128)} %param.43) | copy-start | bytes 1769476
  374.2 21.2 %copy-start.9 = (f32[2,384,192]{1,2,0:T(8,128)S(1)}, f32[2,384,192]{1,2,0:T(8,128)}, u32[]{:S(2)}) copy-start(f32[2,384,192]{1,2,0:T(8,128)} %param.44) | copy-start | bytes 1769476
  374.2 21.2 %copy-start.16 = (f32[192,384]{1,0:T(8,128)S(1)}, f32[192,384]{1,0:T(8,128)}, u32[]{:S(2)}) copy-start(f32[192,384]{1,0:T(8,128)} %get-tuple-element.178) | copy-start | bytes 884740
  374.2 21.2 %copy-start.17 = (f32[192,384]{1,0:T(8,128)S(1)}, f32[192,384]{1,0:T(8,128)}, u32[]{:S(2)}) copy-start(f32[192,384]{1,0:T(8,128)} %get-tuple-element.179) | copy-start | bytes 884740
  394.9 4.2 %collective-permute-start.1 = (f32[2,48,768]{2,1,0:T(8,128)S(1)}, f32[2,48,768]{2,1,0:T(8,128)S(1)}, u32[]{:S(2)}, u32[]{:S(2)}) collective-permute-start(f32[2,48,768]{2,1,0:T(8,128)S(1)} %pad_maximum_fusion), channel_id=1, source_target_pairs={{0,1},{1,0},{2,3},{3,2},{4,5},{5,4},{6,7},{7,6},{8,9},{9,8},{10,11... | collective-permute-start | bytes 884744 | tf_op jit(solution)/shard_map/ppermute | solution.py:1132
  395.4 2.2 copy-start.2
  395.4 2.2 copy-start.10
  395.4 2.2 copy-start.11
  395.4 2.2 copy-start.14
  395.4 2.2 copy-start.15
  397.6 1.7 copy-start.6
  397.6 1.6 copy-start.18
  397.7 1.6 copy-start.19
  400.7 1.9 copy-start.4
  402.7 2.0 copy-start.5
  (5 other events, 7.1 us)
